TPU v7x, 256 devices: a whole 4x4x8 slice. The times are simulated.
256 devices in a mesh: mem: 8 (over x, core), grid: 32 (over y, z).
Axes of the slice: x: 4, y: 4, z: 8, core: 2. Of those that a mesh axis runs over, the one named last changes fastest.
Arguments:
- prior: float32 [320, 2, 16, 2, 1280], P('grid', None, 'mem'), may hold values from -120 to 120
- posterior: float32 [320, 2, 16, 2, 1280], P('grid', None, 'mem'), may hold values from -120 to 120
- cycle_rows: int32 [320], replicated, may hold values from 0 to 319, each once
- relaxation: float32 [2], replicated, may hold values from 0.3 to 0.95
Outputs:
- inflated: float32 [320, 2, 16, 2, 1280], P('grid', None, 'mem')
All inputs are finite; a program needn't handle non-finite values.
Results may differ from a plain program's by a relative error of at most 0.0023.
Values sent between devices are 32-bit elements; how exact they have to be, the bound alone decides.
A program may use at most 192 MiB of HBM per device.

v0:
```python
import math

import jax
import jax.numpy as jnp
from jax import lax
from jax.sharding import PartitionSpec as P

precise = lax.Precision.HIGHEST
epsilon = 1e-06


def cycle_terms(cycle_rows, orders):
    colatitude = math.pi * (cycle_rows.astype(jnp.float32) + 0.5) / orders
    sine_values = jnp.sin(colatitude)
    return (jnp.cos(colatitude), sine_values, math.pi / orders * sine_values)


def fourier_angles(grid_count, half_slots, longitudes):
    orders = longitudes // 2
    owners = jnp.arange(grid_count, dtype=jnp.int32)[:, None]
    slot_ids = jnp.arange(2 * half_slots, dtype=jnp.int32)[None, :]
    base_ids = owners * half_slots + slot_ids
    order_ids = jnp.where(slot_ids < half_slots, base_ids, orders - 1 - (base_ids - half_slots))
    points = jnp.arange(longitudes, dtype=jnp.int32)
    phases = points[:, None, None] * order_ids[None, :, :] % longitudes
    angles = 2.0 * math.pi / longitudes * phases.astype(jnp.float32)
    return (order_ids, angles)


def forward_table(angles, longitudes):
    return jnp.stack([jnp.cos(angles), -jnp.sin(angles)], axis=-1).reshape(longitudes, -1)


def inverse_table(order_ids, angles, longitudes):
    weight = jnp.where(order_ids == 0, 1.0, 2.0).astype(angles.dtype)[None, :, :] / longitudes
    stacked = jnp.stack([weight * jnp.cos(angles), -weight * jnp.sin(angles)], axis=-1)
    return jnp.transpose(stacked, (1, 2, 3, 0)).reshape(-1, longitudes)


def legendre_table(pair_ids, cosines, sine_values, orders):
    row_count = orders // 2 + 1
    pair_count = pair_ids.shape[0]
    cycle_count = cosines.shape[0]
    positions = jnp.arange(1, orders + 1).astype(cosines.dtype)
    cumulative_log = jnp.concatenate(
        [
            jnp.zeros((1,), cosines.dtype),
            jnp.cumsum(jnp.log((2.0 * positions - 1.0) / (2.0 * positions))),
        ]
    )
    all_orders = jnp.arange(orders + 1, dtype=jnp.int32)
    log_sine = jnp.log(sine_values)
    second_order = orders - 1 - pair_ids
    first_length = orders - pair_ids

    def start_log(order_ids):
        matches = all_orders[None, :] == order_ids[:, None]
        partial_log = jnp.sum(jnp.where(matches, cumulative_log[None, :], 0.0), axis=1)
        order_real = order_ids.astype(cosines.dtype)
        leading_log = 0.5 * (jnp.log((2.0 * order_real + 1.0) / 2.0) + partial_log)
        return leading_log[:, None] + order_real[:, None] * log_sine[None, :]

    start_first = start_log(pair_ids)
    start_second = start_log(second_order)
    rescale_log = 18.0 * math.log(10.0)

    def advance(recurrence_state, row_index):
        previous, earlier, scale_log = recurrence_state
        in_first = row_index < first_length
        order_now = jnp.where(in_first, pair_ids, second_order)
        degree_now = jnp.where(in_first, pair_ids + row_index, row_index - 1)
        restart = ((row_index == 0) | (row_index == first_length))[:, None]
        degree_real = degree_now.astype(cosines.dtype)[:, None]
        order_real = order_now.astype(cosines.dtype)[:, None]
        difference = jnp.maximum(degree_real * degree_real - order_real * order_real, 1.0)
        leading = jnp.sqrt((4.0 * degree_real * degree_real - 1.0) / difference)
        lower = degree_real - 1.0
        trailing = jnp.sqrt(
            jnp.maximum(lower * lower - order_real * order_real, 0.0)
            / jnp.maximum(4.0 * lower * lower - 1.0, 1.0)
        )
        current = leading * (cosines[None, :] * previous - trailing * earlier)
        current = jnp.where(restart, 1.0, current)
        earlier = jnp.where(restart, 0.0, previous)
        scale_log = jnp.where(
            restart, jnp.where(in_first[:, None], start_first, start_second), scale_log
        )
        too_large = jnp.abs(current) > 1e18
        current = jnp.where(too_large, current * 1e-18, current)
        earlier = jnp.where(too_large, earlier * 1e-18, earlier)
        scale_log = jnp.where(too_large, scale_log + rescale_log, scale_log)
        entry = jnp.where(row_index <= orders, current * jnp.exp(scale_log), 0.0)
        return ((current, earlier, scale_log), entry)

    def advance_two(recurrence_state, step_index):
        recurrence_state, upper_row = advance(recurrence_state, 2 * step_index)
        recurrence_state, lower_row = advance(recurrence_state, 2 * step_index + 1)
        return (recurrence_state, jnp.stack([upper_row, lower_row], axis=0))

    empty_state = jnp.zeros((pair_count, cycle_count), cosines.dtype)
    final_state, legendre = lax.scan(
        advance_two,
        (empty_state, empty_state, empty_state),
        jnp.arange(row_count, dtype=jnp.int32),
        unroll=4,
    )
    return legendre


def first_rows(pair_ids, row_count, orders):
    row_ids = (
        2 * jnp.arange(row_count, dtype=jnp.int32)[None, :]
        + jnp.arange(2, dtype=jnp.int32)[:, None]
    )
    return row_ids[None, :, :] < (orders - pair_ids)[:, None, None]


def analyse(fourier, legendre, pair_ids, weights, orders):
    half = fourier.shape[0] // 2
    northern = fourier[:, :, :, 0]
    southern = fourier[:, :, :, 1]
    factor = weights[None, None, :, None]
    even_part = (northern + southern) * factor
    odd_part = (northern - southern) * factor
    odd_pairs = (pair_ids % 2 == 1)[:, None, None, None]
    upper_rows = jnp.stack(
        [even_part[:half], jnp.where(odd_pairs, odd_part[half:], even_part[half:])], axis=1
    )
    lower_rows = jnp.stack(
        [odd_part[:half], jnp.where(odd_pairs, even_part[half:], odd_part[half:])], axis=1
    )
    stacked = jnp.stack([upper_rows, lower_rows], axis=1)
    result = jnp.einsum("ieqn,qewrnc->qeiwrc", legendre, stacked, precision=precise)
    in_first = first_rows(pair_ids, legendre.shape[0], orders)[:, :, :, None, None]
    return jnp.where(in_first, result[:, :, :, 0], result[:, :, :, 1])


def synthesise(spectral, legendre, pair_ids, orders):
    in_first = first_rows(pair_ids, legendre.shape[0], orders)[:, :, :, None, None]
    placed = jnp.stack(
        [jnp.where(in_first, spectral, 0.0), jnp.where(in_first, 0.0, spectral)], axis=2
    )
    result = jnp.einsum("ieqn,qewirc->qewrnc", legendre, placed, precision=precise)
    odd_pairs = (pair_ids % 2 == 1)[:, None, None, None]
    even_part = jnp.concatenate(
        [result[:, 0, 0], jnp.where(odd_pairs, result[:, 1, 1], result[:, 0, 1])], axis=0
    )
    odd_part = jnp.concatenate(
        [result[:, 1, 0], jnp.where(odd_pairs, result[:, 0, 1], result[:, 1, 1])], axis=0
    )
    return jnp.stack([even_part + odd_part, even_part - odd_part], axis=3)


def degree_power(spectral, pair_ids, orders, levels):
    pair_count, parity, row_count, parts, columns = spectral.shape
    row_span = 2 * row_count
    squares = jnp.sum(
        (spectral * spectral).reshape(pair_count, 2, row_count, 2, columns // levels, levels),
        axis=(3, 4),
    )
    flattened = jnp.transpose(squares, (0, 3, 2, 1)).reshape(pair_count, levels, row_span)
    row_ids = jnp.arange(row_span, dtype=jnp.int32)
    in_first = (row_ids[None, :] < (orders - pair_ids)[:, None])[:, None, :]
    first_weight = jnp.where(pair_ids == 0, 1.0, 2.0).astype(flattened.dtype)[:, None, None]
    first_part = jnp.where(in_first, flattened, 0.0) * first_weight
    second_part = jnp.where(in_first, 0.0, flattened) * 2.0
    padded = jnp.concatenate(
        [jnp.zeros((pair_count, levels, orders), flattened.dtype), first_part], axis=2
    )

    def shift(segment, offset):
        return lax.dynamic_slice_in_dim(segment, offset, orders, 1)

    shifted = jax.vmap(shift)(padded, orders - pair_ids)
    return jnp.sum(shifted, axis=0) + jnp.sum(second_part[:, :, 1 : orders + 1], axis=0)


def scale_rows(spectral, inflation_ratio, pair_ids, orders):
    pair_count, parity, row_count, parts, columns = spectral.shape
    levels = inflation_ratio.shape[0]
    row_span = 2 * row_count
    ratio_tail = jnp.concatenate(
        [inflation_ratio, jnp.zeros((levels, row_span), inflation_ratio.dtype)], axis=1
    )

    def pick(offset):
        return lax.dynamic_slice_in_dim(ratio_tail, offset, row_span, 1)

    first_part = jax.vmap(pick)(pair_ids)
    edge = jnp.zeros((levels, 1), inflation_ratio.dtype)
    second_part = jnp.concatenate([edge, inflation_ratio, edge], axis=1)
    row_ids = jnp.arange(row_span, dtype=jnp.int32)
    in_first = (row_ids[None, :] < (orders - pair_ids)[:, None])[:, None, :]
    per_row = jnp.where(in_first, first_part, second_part[None, :, :])
    per_row = jnp.transpose(per_row.reshape(pair_count, levels, row_count, 2), (0, 3, 2, 1))
    shaped = spectral.reshape(pair_count, 2, row_count, 2, columns // levels, levels)
    return (shaped * per_row[:, :, :, None, None, :]).reshape(spectral.shape)


def inflation(power_prior, power_post, relaxation, total_members, orders):
    degrees = jnp.arange(orders).astype(power_prior.dtype)[None, :]
    samples = total_members * (2.0 * degrees + 1.0)
    spread_ratio = (power_prior / samples + epsilon) / (power_post / samples + epsilon)
    return (1.0 - relaxation)[:, None] + relaxation[:, None] * jnp.sqrt(spread_ratio)


def per_device(prior, posterior, cycle_rows, relaxation):
    cycle_pairs, halves, members, levels, longitudes = prior.shape
    grid_count = lax.axis_size("grid")
    total_members = members * lax.axis_size("mem")
    orders = longitudes // 2
    half_slots = orders // (2 * grid_count)
    grid_place = lax.axis_index("grid")
    pair_ids = grid_place * half_slots + jnp.arange(half_slots, dtype=jnp.int32)
    columns = members * levels
    local_rows = cycle_pairs * halves * columns
    contract_dims = (((0,), (1,)), ((), ()))
    member_sums = lax.psum((jnp.sum(prior, axis=2), jnp.sum(posterior, axis=2)), "mem")
    mean_prior = member_sums[0] / total_members
    mean_post = member_sums[1] / total_members
    order_ids, angles = fourier_angles(grid_count, half_slots, longitudes)
    forward = forward_table(angles, longitudes)

    def transform(values, centre_values):
        centred = (values - centre_values[:, :, None]).reshape(-1, longitudes)
        return lax.dot_general(forward, centred, contract_dims, precision=precise)

    cosines, sine_values, weights = cycle_terms(cycle_rows, orders)
    legendre = legendre_table(pair_ids, cosines, sine_values, orders)

    def to_slots(arrived):
        return arrived.reshape(2 * half_slots, 2, grid_count * cycle_pairs, halves, columns)

    fourier_prior = transform(prior, mean_prior)
    fourier_post = transform(posterior, mean_post)
    arrived_prior, arrived_post = (
        lax.all_to_all(fourier_prior, "grid", split_axis=0, concat_axis=1, tiled=True),
        lax.all_to_all(fourier_post, "grid", split_axis=0, concat_axis=1, tiled=True),
    )
    spectral_prior = analyse(to_slots(arrived_prior), legendre, pair_ids, weights, orders)
    spectral_post = analyse(to_slots(arrived_post), legendre, pair_ids, weights, orders)
    power_prior, power_post = lax.psum(
        (
            degree_power(spectral_prior, pair_ids, orders, levels),
            degree_power(spectral_post, pair_ids, orders, levels),
        ),
        ("mem", "grid"),
    )
    inflation_ratio = inflation(power_prior, power_post, relaxation, total_members, orders)
    scaled = scale_rows(spectral_post, inflation_ratio, pair_ids, orders)
    spectral = synthesise(scaled, legendre, pair_ids, orders)
    returned = lax.all_to_all(
        spectral.reshape(4 * half_slots, grid_count * local_rows),
        "grid",
        split_axis=1,
        concat_axis=0,
        tiled=True,
    )
    inverse = inverse_table(order_ids, angles, longitudes)
    grid_values = lax.dot_general(returned, inverse, (((0,), (0,)), ((), ())), precision=precise)
    return (
        grid_values.reshape(cycle_pairs, halves, members, levels, longitudes)
        + mean_post[:, :, None]
    )


def solution(mesh):
    return jax.shard_map(
        per_device,
        mesh=mesh,
        in_specs=(P("grid", None, "mem", None, None), P("grid", None, "mem", None, None), P(), P()),
        out_specs=P("grid", None, "mem", None, None),
        check_vma=False,
    )
```

profile of v0, /device:TPU:1, one launch (start us, length us, event | category | flops | bytes accessed | tf_op | source)
XLA Modules:
  0.0 914.5 jit_solution(3250245969405989950)
XLA Ops:
  6.5 2.0 reduce_sum.107
  8.5 2.0 reduce_sum.106
  13.1 0.7 fusion.205
  14.1 13.8 %fusion.171 = (f32[1280,32,20,1]{0,1,3,2:T(8,128)S(1)}, f32[1280,32,20,1]{0,1,3,2:T(8,128)S(1)}, f32[1280,32,20,1]{0,1,3,2:T(8,128)S(1)}, f32[1280,32,20,1]{0,1,3,2:T(8,128)S(1)}) fusion(s32[32,20]{0,1:T(8,128)S(1)} %subtract_select_fusion.8, f32[32,20]{0,1:T(8,128)S(1)} %get-tuple-element.710, f32[32,20]{0,1:T(8,128)S(1)} %get-tuple-element.709), kind=kLoop, calls=%fused_computation.270 | loop fusion | flops 9830400 | bytes 13114880 | tf_op jit(solution)/shard_map/cos | solution.py:31
  27.9 5.6 pad_maximum_fusion.1
  33.6 10.7 %copy.188 = f32[1280,32,20,2]{0,3,2,1:T(2,128)} copy(f32[1280,32,20,2]{0,1,3,2:T(8,128)} %get-tuple-element.715) | data formatting | bytes 13107200 | tf_op jit(solution)/shard_map/stack | solution.py:31
  44.3 8.7 reshape.1251
  53.0 423.0 %while.26 = (s32[]{:T(128)}, f32[10,320]{1,0:T(8,128)S(1)}, f32[10,320]{1,0:T(8,128)S(1)}, f32[10,320]{1,0:T(8,128)S(1)}, f32[80,4,2,10,320]{4,3,2,1,0:T(8,128)}...) while((s32[]{:T(128)}, f32[10,320]{1,0:T(8,128)S(1)}, ...), condition=%wide.region_5.6_spmd.clone.clone.clone, body=%wide.region_4.5_spmd.clone.clone.clone.sunk | while | flops 905471 | bytes 1155262 | solution.py:101
  476.7 1.2 broadcast_multiply_fusion.1
  479.5 8.1 fusion.239
  487.5 12.2 %all-to-all-start = ((f32[32,40,80]{2,1,0:T(8,128)}), f32[32,40,80]{2,1,0:T(8,128)S(1)}, u32[]{:S(2)}, u32[]{:S(2)}) async-start(f32[32,40,80]{2,1,0:T(8,128)} %fusion.239), calls=%async_computation | async-start | bytes 1310720 | tf_op jit(solution)/shard_map/all_to_all | solution.py:238
  500.3 8.1 fusion.240
  508.3 7.8 all-to-all-done
  516.1 8.4 all-to-all-start.1
  524.5 15.2 %copy.186 = f32[320,2,10,320]{0,3,1,2:T(8,128)} copy(f32[320,2,10,320]{3,2,1,0:T(8,128)} %bitcast.223) | data formatting | bytes 16384000 | tf_op jit(solution)/shard_map/reshape | solution.py:101
  539.7 2.3 copy.187
  542.1 0.9 broadcast_compare_fusion.8
  543.3 11.8 %reshape.1255 = f32[20,2,320,2,4]{4,3,2,1,0:T(2,128)} reshape(f32[40,32,80]{2,1,0:T(8,128)S(1)} %copy.197) | data formatting | bytes 819200 | tf_op jit(solution)/shard_map/reshape | solution.py:232
  555.1 14.7 %fusion.238 = (f32[20,2,320,1,4]{4,3,2,1,0:T(1,128)}, f32[20,2,320,1,4]{4,3,2,1,0:T(1,128)}) fusion(f32[20,2,320,2,4]{4,3,2,1,0:T(2,128)} %reshape.1255), kind=kLoop, calls=%fused_computation.424 | loop fusion | bytes 819200 | tf_op jit(solution)/shard_map/slice | solution.py:121
  569.8 11.7 %copy.235 = f32[20,2,320,1,4]{2,4,1,0,3:T(4,128)S(1)} copy(f32[20,2,320,1,4]{4,3,2,1,0:T(1,128)} %get-tuple-element.674) | data formatting | bytes 409600
  581.5 11.7 %copy.234 = f32[20,2,320,1,4]{2,4,1,0,3:T(4,128)S(1)} copy(f32[20,2,320,1,4]{4,3,2,1,0:T(1,128)} %get-tuple-element.675) | data formatting | bytes 409600
  593.2 11.8 %reshape.1253 = f32[20,2,320,2,4]{4,3,2,1,0:T(2,128)} reshape(f32[40,32,80]{2,1,0:T(8,128)S(1)} %copy.192) | data formatting | bytes 819200 | tf_op jit(solution)/shard_map/reshape | solution.py:232
  605.0 14.7 %fusion.237 = (f32[20,2,320,1,4]{4,3,2,1,0:T(1,128)}, f32[20,2,320,1,4]{4,3,2,1,0:T(1,128)}) fusion(f32[20,2,320,2,4]{4,3,2,1,0:T(2,128)} %reshape.1253), kind=kLoop, calls=%fused_computation.423 | loop fusion | bytes 819200 | tf_op jit(solution)/shard_map/slice | solution.py:121
  619.7 11.7 %copy.233 = f32[20,2,320,1,4]{2,4,1,0,3:T(4,128)S(1)} copy(f32[20,2,320,1,4]{4,3,2,1,0:T(1,128)} %get-tuple-element.672) | data formatting | bytes 409600
  631.4 11.8 %copy.232 = f32[20,2,320,1,4]{2,4,1,0,3:T(4,128)S(1)} copy(f32[20,2,320,1,4]{4,3,2,1,0:T(1,128)} %get-tuple-element.673) | data formatting | bytes 409600
  643.8 1.3 copy-done
  645.1 10.7 %fusion.154 = f32[10,2,321,2,2,4]{2,5,4,3,1,0:T(4,128)S(1)} fusion(f32[1,2,10,320]{0,3,1,2:T(8,128)S(1)} %copy-done, f32[320,2,10,320]{0,3,1,2:T(8,128)} %copy.186, f32[10,1,2,2,320,4]{4,5,3,0,2,1:T(4,128)S(1)} %maximum_bitcast_fusion.9, f32[10,1,2,2,320,4]{4,5,3,0,2,1:T(4,128)S(1)} %maximum_bitcast_fusion.8), kind=kOutput, calls=%fused_computation.245 | convolution fusion | flops 396601600 | bytes 9038080 | tf_op jit(solution)/shard_map/ieqn,qewrnc->qeiwrc/dot_general | solution.py:133
  655.9 6.2 fusion.156
  662.1 0.8 copy-done.4
  663.4 4.5 copy.206
  667.9 4.4 copy.202
  672.3 8.0 fusion.165
  680.6 9.3 %select_multiply_fusion.2 = (f32[10,2,642]{1,0,2:T(8,128)S(1)}, f32[10,2,642]{1,0,2:T(8,128)}) fusion(f32[10]{0:T(128)S(1)} %get-tuple-element.717, pred[10,642]{0,1:T(8,128)(4,1)S(1)} %iota_compare_fusion, f32[10,2,321,2]{1,0,3,2:T(8,128)} %copy.202, f32[10,2,321,2]{1,0,3,2:T(8,128)} %copy.206), kind=kLoop, calls=%fused_computation.256 | loop fusion | flops 51360 | bytes 211900 | tf_op jit(solution)/shard_map/mul | solution.py:165
  689.9 5.8 concatenate.79
  695.7 9.5 %gather_fusion = f32[10,2,640]{1,0,2:T(8,128)} fusion(f32[10,2,1282]{1,0,2:T(8,128)} %concatenate.79, s32[10]{0:T(128)S(1)} %or_bitcast_fusion), kind=kCustom, calls=%fused_computation | custom fusion | bytes 102520 | tf_op jit(solution)/shard_map/vmap()/gather | solution.py:172
  705.2 3.6 reduce_sum.111
  709.5 5.8 concatenate.81
  715.3 9.6 %gather_fusion.1 = f32[10,2,640]{1,0,2:T(8,128)} fusion(f32[10,2,1282]{1,0,2:T(8,128)} %concatenate.81, s32[10]{0:T(128)S(1)} %or_bitcast_fusion), kind=kCustom, calls=%fused_computation.1 | custom fusion | bytes 102520 | tf_op jit(solution)/shard_map/vmap()/gather | solution.py:172
  724.9 4.3 reduce_sum.116
  729.2 1.7 copy.207
  732.3 77.9 %all-reduce.5 = (f32[2,640]{1,0:T(2,128)S(1)}, f32[2,640]{1,0:T(2,128)}) all-reduce(f32[2,640]{1,0:T(2,128)S(1)} %add.1167, f32[2,640]{1,0:T(2,128)S(1)} %add.1163), channel_id=1, replica_groups=mesh['mem'=8,'grid'=32] {'mem','grid'}, use_global_device_ids=true, to_apply=%region_19.20 | all-reduce | flops 2560 | bytes 20480 | tf_op jit(solution)/shard_map/psum | solution.py:242
  810.2 0.8 multiply_add_fusion.5
  811.1 13.2 %while.25 = (s32[]{:T(128)}, f32[2,1282]{1,0:T(2,128)S(1)}, s32[10,2]{0,1:T(2,128)S(1)}, f32[10,2,642]{2,1,0:T(2,128)S(1)}, s32[]{:T(128)}) while((s32[]{:T(128)}, f32[2,1282]{1,0:T(2,128)S(1)}, s32[10,2]{0,1:T(2,128)S(1)}, f32[10,2,642]{2,1,0:T(2,128)S(1)}, s32[]{:T(128)}) %tuple.196), condition=%wide.while_cond, body=%wide.while_body.sunk | while | flops 2 | bytes 12393 | solution.py:187
  811.7 0.7 bitcast_dynamic-update-slice_fusion.2
  813.0 0.7 bitcast_dynamic-update-slice_fusion.2
  814.3 0.7 bitcast_dynamic-update-slice_fusion.2
  815.7 0.7 bitcast_dynamic-update-slice_fusion.2
  817.0 0.7 bitcast_dynamic-update-slice_fusion.2
  820.9 0.7 bitcast_dynamic-update-slice_fusion.2
  824.3 0.9 broadcast_in_dim.703
  825.2 3.7 copy.211
  828.9 1.2 copy.210
  830.1 2.6 select_bitcast_fusion.8
  832.7 1.3 copy.212
  834.3 1.2 broadcast_select_fusion.1
  835.5 12.7 %fusion.179 = f32[10,2,2,2,320,4]{4,5,3,0,2,1:T(4,128)S(1)} fusion(f32[1,2,10,320]{0,3,1,2:T(8,128)S(1)} %copy-done.1, f32[320,2,10,320]{0,3,1,2:T(8,128)} %copy.186, f32[10,2,1,321,2,4]{3,5,4,1,0,2:T(4,128)S(1)} %get-tuple-element.677, f32[10,2,1,321,2,4]{3,5,4,1,0,2:T(4,128)S(1)} %get-tuple-element.676), kind=kOutput, calls=%fused_computation.277 | convolution fusion | flops 396601920 | bytes 9038080 | tf_op jit(solution)/shard_map/ieqn,qewirc->qewrnc/dot_general | solution.py:143
  848.6 11.5 %copy.215 = f32[20,2,320,2,4]{4,3,2,1,0:T(2,128)} copy(f32[20,2,320,2,4]{2,4,1,0,3:T(4,128)S(1)} %pad_maximum_fusion.6) | data formatting | bytes 819200 | tf_op jit(solution)/shard_map/stack | solution.py:151
  860.2 12.0 %all_to_all.38 = f32[40,32,80]{2,1,0:T(8,128)S(1)} reshape(f32[20,2,320,2,4]{4,3,2,1,0:T(2,128)} %copy.215) | data formatting | bytes 819200 | tf_op jit(solution)/shard_map/all_to_all | solution.py:252
  872.2 1.2 copy.216
  873.4 6.8 all-to-all-start.2
  880.1 10.7 %copy.218 = f32[32,20,2,1280]{3,2,1,0:T(2,128)} copy(f32[32,20,2,1280]{3,0,2,1:T(8,128)} %get-tuple-element.716) | data formatting | bytes 13107200 | tf_op jit(solution)/shard_map/transpose | solution.py:37
  890.8 8.7 reshape.1293
  900.0 6.3 fusion.176
  906.4 1.1 copy.220
  (2693 shorter events, 224.3 us)
Async XLA Ops:
  6.5 470.1 %all-reduce.9.cloned.1.call-start = ((), (), s32[]{:S(2)}) async-start(), calls=%async_computation.3 | async-start | bytes 819200 | tf_op jit(solution)/shard_map/psum | solution.py:218
  12.0 631.4 %copy-start.7 = (pred[10]{0:T(512)(128)(4,1)}, pred[10]{0:T(512)(128)(4,1)S(1)}, u32[]{:S(2)}) copy-start(pred[10]{0:T(512)(128)(4,1)S(1)} %get-tuple-element.721) | copy-start | bytes 34
  53.0 423.2 %copy-start.9 = (f32[2]{0:T(128)S(1)}, f32[2]{0:T(128)}, u32[]{:S(2)}) copy-start(f32[2]{0:T(128)} %param.9) | copy-start | bytes 28
  53.0 425.7 %copy-start.5 = (f32[10,2,2,2,1280]{4,3,2,1,0:T(2,128)S(1)}, f32[10,2,2,2,1280]{4,3,2,1,0:T(2,128)}, u32[]{:S(2)}) copy-start(f32[10,2,2,2,1280]{4,3,2,1,0:T(2,128)} %param.7) | copy-start | bytes 1228804
  477.9 21.9 %copy-start.6 = (f32[10,2,2,2,1280]{4,3,2,1,0:T(2,128)S(1)}, f32[10,2,2,2,1280]{4,3,2,1,0:T(2,128)}, u32[]{:S(2)}) copy-start(f32[10,2,2,2,1280]{4,3,2,1,0:T(2,128)} %param.6) | copy-start | bytes 1228804
  478.0 0.7 copy-start.2
  487.5 28.6 %all-to-all-start = ((f32[32,40,80]{2,1,0:T(8,128)}), f32[32,40,80]{2,1,0:T(8,128)S(1)}, u32[]{:S(2)}, u32[]{:S(2)}) async-start(f32[32,40,80]{2,1,0:T(8,128)} %fusion.239), calls=%async_computation | async-start | bytes 1310720 | tf_op jit(solution)/shard_map/all_to_all | solution.py:238
  516.1 27.0 %all-to-all-start.1 = ((f32[32,40,80]{2,1,0:T(8,128)}), f32[32,40,80]{2,1,0:T(8,128)S(1)}, u32[]{:S(2)}, u32[]{:S(2)}) async-start(f32[32,40,80]{2,1,0:T(8,128)} %fusion.240), calls=%async_computation.1 | async-start | bytes 1310720 | tf_op jit(solution)/shard_map/all_to_all | solution.py:237
  631.4 24.4 %slice-start = ((s8[9830400]{0:T(1024)(128)(4,1)}), s8[1441792]{0:T(1024)(128)(4,1)S(1)}, s32[]{:S(2)}) async-start(s8[9830400]{0:T(1024)(128)(4,1)} %bitcast.217), calls=%async_computation.4 | async-start | bytes 2883584
  643.2 1.9 copy-start
  643.4 12.4 %slice-start.1 = ((s8[9830400]{0:T(1024)(128)(4,1)}), s8[4194304]{0:T(1024)(128)(4,1)S(1)}, s32[]{:S(2)}) async-start(s8[9830400]{0:T(1024)(128)(4,1)} %bitcast.217), calls=%async_computation.5 | async-start | bytes 8388608
  645.1 10.7 %slice-start.2 = ((s8[9830400]{0:T(1024)(128)(4,1)}), s8[4194304]{0:T(1024)(128)(4,1)S(1)}, s32[]{:S(2)}) async-start(s8[9830400]{0:T(1024)(128)(4,1)} %bitcast.217), calls=%async_computation.6 | async-start | bytes 8388608
  662.1 0.8 copy-start.4
  715.3 120.2 %copy-start.1 = (f32[1,2,10,320]{0,3,1,2:T(8,128)S(1)}, f32[1,2,10,320]{0,3,1,2:T(8,128)}, u32[]{:S(2)}) copy-start(f32[1,2,10,320]{0,3,1,2:T(8,128)} %copy.187) | copy-start | bytes 76804
  835.5 12.8 %copy-start.8 = (pred[10]{0:T(512)(128)(4,1)S(1)}, pred[10]{0:T(512)(128)(4,1)}, u32[]{:S(2)}) copy-start(pred[10]{0:T(512)(128)(4,1)} %copy-done.7) | copy-start | bytes 34
  873.4 26.2 %all-to-all-start.2 = ((f32[40,32,80]{2,0,1:T(8,128)}), f32[40,32,80]{2,0,1:T(8,128)S(1)}, u32[]{:S(2)}, u32[]{:S(2)}) async-start(f32[40,32,80]{2,0,1:T(8,128)} %copy.216), calls=%async_computation.2 | async-start | bytes 1310720 | tf_op jit(solution)/shard_map/all_to_all | solution.py:252
  890.8 9.2 %copy-start.3 = (f32[10,2,2,1280]{3,0,2,1:T(8,128)S(1)}, f32[10,2,2,1280]{3,0,2,1:T(8,128)}, u32[]{:S(2)}) copy-start(f32[10,2,2,1280]{3,0,2,1:T(8,128)} %copy-done.2) | copy-start | bytes 614404
Sparse Core Ops, SparseCore 0:
  10.6 67.3 all-reduce.8
where the time goes:
time: 927 us; the launch traced here: 914 us
  local copies, waits for them, and re-layouts  304 us (33%)
  loops' own time  217 us (23%)
  other arithmetic  213 us (23%)
  blocking collectives  77.9 us (8%)
  matrix products  52.1 us (6%)
  starting transfers between devices  27.4 us (3%)
  between operations  14.9 us (2%)
    another operation x1, loops' own time, legendre_table(): lax.scan(advance_two, (empty_state, empty_state, empty_state), jnp.arange...  217 us
    psum x1, blocking collectives, per_device(): lax.psum((degree_power(spectral_prior, pair_ids, orders, levels), degree_...  77.9 us
    another operation x641, other arithmetic, advance_two(): return (recurrence_state, jnp.stack([upper_row, lower_row], axis=0))  67.3 us
    dynamic_update_slice x80, other arithmetic, legendre_table(): lax.scan(advance_two, (empty_state, empty_state, empty_state), jnp.arange...  56.1 us
    slice x81, local copies, waits for them, and re-layouts, legendre_table(): lax.scan(advance_two, (empty_state, empty_state, empty_state), jnp.arange...  54.1 us
    unnamed x30, local copies, waits for them, and re-layouts  49.7 us
    slice x2, local copies, waits for them, and re-layouts, analyse(): southern = fourier[:, :, :, 1]  29.5 us
    reshape x2, local copies, waits for them, and re-layouts, to_slots(): arrived.reshape(2 * half_slots, 2, grid_count * cycle_pairs, halves, colu...  23.7 us
  transfers between devices with their start and end apart: 4, of which 1 were waited for; matrix products, arithmetic and copies ran while one was open for 32% of the time, Pallas kernels for 0%

commit v1 on v0

v1 whole, which is shorter than its diff:
```python
import functools
import math

import jax
import jax.numpy as jnp
import ml_dtypes
import numpy as np
from jax import lax
from jax.experimental import pallas as pl
from jax.experimental.pallas import tpu as pltpu
from jax.sharding import PartitionSpec as P

MESH = pl.DeviceIdType.MESH
NLAT = 640
LEV = 2
NLON = 1280
NPAIR = 320
MEMBERS = 16
NG = 32
NM = 8
NY = 4
NZ = 8
HALF = 10
EPS = 1e-06
ROWS = 672
TROWS = 384
BIG = 60 * 1024 * 1024

f32 = jnp.float32
bf16 = jnp.bfloat16


def split_table(table):
    hi = table.astype(np.float32).astype(ml_dtypes.bfloat16)
    lo = (table - hi.astype(np.float64)).astype(np.float32).astype(ml_dtypes.bfloat16)
    return hi, lo


@functools.lru_cache(maxsize=None)
def trig_tables():
    owner = np.arange(NG)[:, None, None]
    pair = np.arange(HALF)[None, :, None]
    segment = np.arange(2)[None, None, :]
    first = owner * HALF + pair
    order = np.where(segment == 0, first, NLAT - 1 - first).reshape(-1)
    phase = (np.arange(NLON)[:, None] * order[None, :]) % NLON
    angle = 2.0 * np.pi / NLON * phase
    table = np.stack([np.cos(angle), -np.sin(angle)], axis=-1).reshape(NLON, NLON)
    weight = np.repeat(np.where(order == 0, 1.0, 2.0) / NLON, 2)
    return split_table(table) + split_table((table * weight[None, :]).T)


@functools.lru_cache(maxsize=None)
def leading_logs():
    i = np.arange(1, NLAT + 1, dtype=np.float64)
    total = np.concatenate([[0.0], np.cumsum(np.log((2 * i - 1) / (2 * i)))])[:NLAT]
    m = np.arange(NLAT, dtype=np.float64)
    return (0.5 * (np.log((2 * m + 1) / 2) + total)).astype(np.float32)


def means_kernel(prior_ref, post_ref, mean_ref, sums, arrived, piece, s1, r1, s2, r2):
    me = lax.axis_index("mem")
    barrier = pltpu.get_barrier_semaphore()
    for k in range(1, NM):
        pl.semaphore_signal(
            barrier, inc=1, device_id={"mem": lax.rem(me + k, NM)}, device_id_type=MESH
        )
    for ens, ref in ((0, prior_ref), (1, post_ref)):
        for j in range(HALF):
            for h in range(2):
                sums[ens * 20 + j * 2 + h] = ref[j, h, 0] + ref[j, h, 1]
    pl.semaphore_wait(barrier, NM - 1)
    copies = []
    for k in range(1, NM):
        peer = lax.rem(me + k, NM)
        copy = pltpu.make_async_remote_copy(
            src_ref=sums.at[pl.ds(peer * 5, 5)],
            dst_ref=arrived.at[NM - 1 - k],
            send_sem=s1.at[k - 1],
            recv_sem=r1.at[k - 1],
            device_id={"mem": peer},
            device_id_type=MESH,
        )
        copy.start()
        copies.append(copy)
    total = sums[pl.ds(me * 5, 5)]
    for k, copy in enumerate(copies):
        copy.wait_recv()
        total = total + arrived[NM - 2 - k]
    piece[...] = total * (1.0 / MEMBERS)
    mean_ref[pl.ds(me * 5, 5)] = piece[...]
    back = []
    for k in range(1, NM):
        peer = lax.rem(me + k, NM)
        copy = pltpu.make_async_remote_copy(
            src_ref=piece,
            dst_ref=mean_ref.at[pl.ds(me * 5, 5)],
            send_sem=s2.at[k - 1],
            recv_sem=r2.at[k - 1],
            device_id={"mem": peer},
            device_id_type=MESH,
        )
        copy.start()
        back.append(copy)
    for copy in copies:
        copy.wait_send()
    for copy in back:
        copy.wait()


def member_means(prior, posterior):
    return pl.pallas_call(
        means_kernel,
        out_shape=jax.ShapeDtypeStruct((40, LEV, NLON), f32),
        in_specs=[pl.BlockSpec(memory_space=pltpu.VMEM)] * 2,
        out_specs=pl.BlockSpec(memory_space=pltpu.VMEM),
        scratch_shapes=[
            pltpu.VMEM((40, LEV, NLON), f32),
            pltpu.VMEM((NM - 1, 5, LEV, NLON), f32),
            pltpu.VMEM((5, LEV, NLON), f32),
            pltpu.SemaphoreType.DMA((NM - 1,)),
            pltpu.SemaphoreType.DMA((NM - 1,)),
            pltpu.SemaphoreType.DMA((NM - 1,)),
            pltpu.SemaphoreType.DMA((NM - 1,)),
        ],
        compiler_params=pltpu.CompilerParams(
            collective_id=0, has_side_effects=True, vmem_limit_bytes=BIG
        ),
        name="member_means",
    )(prior, posterior)


def legendre_kernel(start_ref, cosine_ref, place_ref, table_ref, rows):
    place = place_ref[0]
    zero = jnp.zeros((16, TROWS), f32)
    for i in range(641, ROWS):
        for t in range(3):
            rows[t, i * 16 : i * 16 + 16, :] = zero[:, 0:128]
    sub = lax.broadcasted_iota(jnp.int32, (16, 128), 0)
    step = lax.rem(lax.broadcasted_iota(jnp.int32, (16, 128), 1), 8)
    cosine = jnp.broadcast_to(cosine_ref[...], (16, TROWS))
    pair = place * HALF + sub
    valid = sub < HALF

    def chain(segment, first_block, order):
        def block(b, state):
            current, earlier, scale_log = state
            degree = (b * 8 + step).astype(f32)
            m = order.astype(f32)
            inside = valid & (b * 8 + step > order)
            square = degree * degree
            difference = jnp.where(inside, square - m * m, 1.0)
            low = degree - 1.0
            low_square = low * low
            lead = (4.0 * square - 1.0) / difference
            trail = jnp.maximum(low_square - m * m, 0.0) / jnp.maximum(4.0 * low_square - 1.0, 1.0)
            a = jnp.where(inside, jnp.sqrt(jnp.maximum(lead, 0.0)), 0.0)
            c = jnp.where(inside, a * jnp.sqrt(trail), 0.0)
            d = jnp.where(valid & (b * 8 + step == order), 1.0, 0.0)
            scale = jnp.exp(scale_log)
            for k in range(8):
                ak = jnp.broadcast_to(a[:, k : k + 1], (16, TROWS))
                ck = jnp.broadcast_to(c[:, k : k + 1], (16, TROWS))
                dk = jnp.broadcast_to(d[:, k : k + 1], (16, TROWS))
                following = (ak * cosine) * current + (dk - ck * earlier)
                earlier = current
                current = following
                entry = current * scale
                degree_now = b * 8 + k
                if segment == 0:
                    offset = pl.multiple_of((NLAT - 1 - degree_now) * 16, 16)
                else:
                    offset = pl.multiple_of((degree_now + 1) * 16, 16)
                    second = degree_now >= NLAT - 1 - pair
                for t in range(3):
                    tile = entry[:, t * 128 : t * 128 + 128]
                    if segment == 1:
                        tile = jnp.where(second, tile, rows[t, pl.ds(offset, 16), :])
                    rows[t, pl.ds(offset, 16), :] = tile
            large = jnp.abs(current) > 1e10
            current = jnp.where(large, current * 1e-20, current)
            earlier = jnp.where(large, earlier * 1e-20, earlier)
            scale_log = jnp.where(large, scale_log + 20.0 * math.log(10.0), scale_log)
            return current, earlier, scale_log

        lax.fori_loop(first_block, NLAT // 8, block, (zero, zero, start_ref[segment]))

    chain(0, lax.div(place * HALF, 8), pair)
    chain(1, lax.div(NLAT - HALF - place * HALF, 8), NLAT - 1 - pair)

    right = lax.broadcasted_iota(jnp.int32, (16, 128), 1) < 64
    blank = jnp.zeros((TROWS - ROWS // 2, 640), bf16)
    for p in range(HALF):
        for q in range(2):

            def convert(t, carry):
                out = pl.ds(pl.multiple_of(t * 16, 16), 16)
                for tile in range(3):
                    values = rows[tile, pl.ds(t * 512 + q * 16 + p, 16, stride=32), :]
                    high = values.astype(bf16)
                    low = values - high.astype(f32)
                    if tile < 2:
                        at = tile * 128
                        table_ref[p * 2 + q, out, at : at + 128] = high
                        table_ref[p * 2 + q, out, at + 256 : at + 384] = low.astype(bf16)
                    else:
                        table_ref[p * 2 + q, out, 512:640] = jnp.where(right, values, low).astype(bf16)
                return carry

            lax.fori_loop(0, ROWS // 32, convert, 0, unroll=3)
            table_ref[p * 2 + q, ROWS // 2 : TROWS, :] = blank


def legendre_table(start, cosine, place):
    return pl.pallas_call(
        legendre_kernel,
        out_shape=jax.ShapeDtypeStruct((2 * HALF, TROWS, 640), bf16),
        in_specs=[
            pl.BlockSpec(memory_space=pltpu.VMEM),
            pl.BlockSpec(memory_space=pltpu.VMEM),
            pl.BlockSpec(memory_space=pltpu.SMEM),
        ],
        out_specs=pl.BlockSpec(memory_space=pltpu.VMEM),
        scratch_shapes=[pltpu.VMEM((3, ROWS * 16, 128), f32)],
        compiler_params=pltpu.CompilerParams(vmem_limit_bytes=BIG),
        name="legendre_table",
    )(start, cosine, place)


def split_rows(values):
    high = values.astype(bf16)
    low = (values - high.astype(f32)).astype(bf16)
    return high, low


def forward_kernel(
    prior_ref, post_ref, mean_ref, high_ref, low_ref, out_a, out_b, left, split
):
    @pl.when(pl.program_id(0) == 0)
    def _():
        left[...] = jnp.zeros_like(left)
        for ens, ref in ((0, prior_ref), (1, post_ref)):
            for j in range(HALF):
                north_mean = mean_ref[ens * 20 + j * 2]
                south_mean = mean_ref[ens * 20 + j * 2 + 1]
                for b in range(2):
                    north = ref[j, 0, b] - north_mean
                    south = ref[j, 1, b] - south_mean
                    for q, part in ((0, north + south), (1, north - south)):
                        for v in range(LEV):
                            row = (q * 8 + ens * 4 + b * 2 + v) * 16 + j
                            left[row : row + 1, :] = part[v : v + 1, :]
        high, low = split_rows(left[...])
        split[0:256, :] = high
        split[256:512, :] = low

    both = jnp.dot(split[...], high_ref[...], preferred_element_type=f32)
    result = both[0:256] + both[256:512]
    result = result + jnp.dot(split[0:256, :], low_ref[...], preferred_element_type=f32)
    for o in range(16):
        block = jnp.concatenate(
            [result[x * 16 : x * 16 + 16, o * 40 : o * 40 + 40] for x in range(16)], axis=1
        )
        out_a[o * 8 : o * 8 + 8, :] = block[0:8]
        out_b[o] = block[8:10]


def forward_fourier(prior, posterior, mean, high, low):
    full = pl.BlockSpec((HALF, 2, 2, LEV, NLON), lambda i: (0, 0, 0, 0, 0))
    return pl.pallas_call(
        forward_kernel,
        grid=(2,),
        out_shape=(
            jax.ShapeDtypeStruct((NG * 8, 640), f32),
            jax.ShapeDtypeStruct((NG, 2, 640), f32),
        ),
        in_specs=[
            full,
            full,
            pl.BlockSpec((40, LEV, NLON), lambda i: (0, 0, 0)),
            pl.BlockSpec((NLON, 640), lambda i: (0, i)),
            pl.BlockSpec((NLON, 640), lambda i: (0, i)),
        ],
        out_specs=(
            pl.BlockSpec((NG * 4, 640), lambda i: (i, 0)),
            pl.BlockSpec((NG // 2, 2, 640), lambda i: (i, 0, 0)),
        ),
        scratch_shapes=[pltpu.VMEM((256, NLON), f32), pltpu.VMEM((512, NLON), bf16)],
        compiler_params=pltpu.CompilerParams(vmem_limit_bytes=BIG),
        name="forward_fourier",
    )(prior, posterior, mean, high, low)


def exchange_kernel(src_a, src_b, dst_a, dst_b, local_sem, send_sem, recv_sem):
    me = lax.axis_index("grid")
    y, z = lax.div(me, NZ), lax.rem(me, NZ)
    barrier = pltpu.get_barrier_semaphore()

    def peer_of(k):
        return lax.rem(y + k // NZ, NY) * NZ + lax.rem(z + k % NZ, NZ)

    def eight(place):
        return pl.ds(pl.multiple_of(place * 8, 8), 8)

    for k in range(1, NG):
        pl.semaphore_signal(barrier, inc=1, device_id={"grid": peer_of(k)}, device_id_type=MESH)
    mine = [
        pltpu.make_async_copy(src_a.at[eight(me), :], dst_a.at[eight(me), :], local_sem.at[0]),
        pltpu.make_async_copy(src_b.at[me], dst_b.at[me], local_sem.at[1]),
    ]
    for copy in mine:
        copy.start()
    pl.semaphore_wait(barrier, NG - 1)
    copies = []
    order = sorted(range(1, NG), key=lambda k: -min(k % NZ, NZ - k % NZ))
    for k in order:
        peer = peer_of(k)
        for part, source, target in (
            (0, src_a.at[eight(peer), :], dst_a.at[eight(me), :]),
            (1, src_b.at[peer], dst_b.at[me]),
        ):
            copy = pltpu.make_async_remote_copy(
                src_ref=source,
                dst_ref=target,
                send_sem=send_sem.at[part, k],
                recv_sem=recv_sem.at[part, k],
                device_id={"grid": peer},
                device_id_type=MESH,
            )
            copy.start()
            copies.append(copy)
    for copy in mine + copies:
        copy.wait()


def exchange(values, collective_id):
    return pl.pallas_call(
        exchange_kernel,
        out_shape=tuple(jax.ShapeDtypeStruct(v.shape, f32) for v in values),
        in_specs=[pl.BlockSpec(memory_space=pltpu.VMEM)] * 2,
        out_specs=(pl.BlockSpec(memory_space=pltpu.VMEM),) * 2,
        scratch_shapes=[
            pltpu.SemaphoreType.DMA((2,)),
            pltpu.SemaphoreType.DMA((2, NG)),
            pltpu.SemaphoreType.DMA((2, NG)),
        ],
        compiler_params=pltpu.CompilerParams(
            collective_id=collective_id, has_side_effects=True, vmem_limit_bytes=BIG
        ),
        name="exchange_%d" % collective_id,
    )(*values)


def analyse_kernel(
    src_a, src_b, weight_ref, place_ref, table_ref, spectral_ref, power_ref, turned, total, pairs
):
    p = pl.program_id(0)

    @pl.when(p == 0)
    def _():
        for g in range(NG):
            two = src_b[g]
            pairs[g * 2 : g * 2 + 2, :] = two
            pairs[64 + g * 2 : 64 + g * 2 + 2, :] = two
        for t in range(2):
            at = t * 128
            turned[t] = src_a[at : at + 128, :].T * weight_ref[:, at : at + 128]
        turned[2] = pairs[...].T * weight_ref[:, 256:384]
        total[...] = jnp.zeros_like(total)

    pair = place_ref[0] * HALF + p
    odd_pair = lax.rem(p, 2)
    lane = lax.broadcasted_iota(jnp.int32, (16, TROWS), 1)
    first_weight = jnp.where(pair == 0, 1.0, 2.0).astype(f32)
    for q in range(2):
        groups = []
        for e in range(2):
            parity = lax.rem(q + odd_pair + 1 - e, 2)
            for part in range(2):
                start = parity * 320 + p * 4 + e * 2 + part
                groups.append(
                    jnp.concatenate(
                        [turned[t, pl.ds(start, 8, stride=40), :] for t in range(3)], axis=1
                    )
                )
        high, low = split_rows(jnp.concatenate(groups, axis=0))
        left = jnp.concatenate(
            [
                jnp.concatenate([high[:, 0:256], high[:, 0:256], high[:, 256:384]], axis=1),
                jnp.concatenate([low[:, 0:256], low[:, 0:256], low[:, 256:384]], axis=1),
            ],
            axis=0,
        )
        both = lax.dot_general(
            left, table_ref[q], (((1,), (1,)), ((), ())), preferred_element_type=f32
        )
        result = both[0:32] + both[32:64]
        in_first = 2 * lane + q < NLAT - pair
        chosen = jnp.where(in_first, result[0:16], result[16:32])
        spectral_ref[q] = chosen
        squares = chosen * chosen
        total[0, :, q * TROWS : (q + 1) * TROWS] += jnp.where(in_first, squares, 0.0) * first_weight
        total[1, :, q * TROWS : (q + 1) * TROWS] += jnp.where(in_first, 0.0, squares) * 2.0

    @pl.when(p == HALF - 1)
    def _():
        for s in range(2):
            merged = total[s, 0:8, :] + total[s, 8:16, :]
            for ens in range(2):
                row = s * 4 + ens * 2
                power_ref[row : row + 2, 0:768] = (
                    merged[ens * 4 : ens * 4 + 2, :] + merged[ens * 4 + 2 : ens * 4 + 4, :]
                )
        power_ref[:, 768:1024] = jnp.zeros((8, 256), f32)


def analyse(arrived, weights, place, table):
    return pl.pallas_call(
        analyse_kernel,
        grid=(HALF,),
        out_shape=(
            jax.ShapeDtypeStruct((2 * HALF, 16, TROWS), f32),
            jax.ShapeDtypeStruct((8, 1024), f32),
        ),
        in_specs=[
            pl.BlockSpec((NG * 8, 640), lambda i: (0, 0)),
            pl.BlockSpec((NG, 2, 640), lambda i: (0, 0, 0)),
            pl.BlockSpec((1, TROWS), lambda i: (0, 0)),
            pl.BlockSpec(memory_space=pltpu.SMEM),
            pl.BlockSpec((2, TROWS, 640), lambda i: (i, 0, 0)),
        ],
        out_specs=(
            pl.BlockSpec((2, 16, TROWS), lambda i: (i, 0, 0)),
            pl.BlockSpec((8, 1024), lambda i: (0, 0)),
        ),
        scratch_shapes=[pltpu.VMEM((3, 640, 128), f32), pltpu.VMEM((2, 16, 2 * TROWS), f32),
            pltpu.VMEM((128, 640), f32),
        ],
        compiler_params=pltpu.CompilerParams(vmem_limit_bytes=BIG),
        name="analyse",
    )(*arrived, weights, place, table)


def power_kernel(src, out, own, at_m, at_y, at_z, s1, r1, s2, r2, s3, r3, s4, r4):
    mem = lax.axis_index("mem")
    grid = lax.axis_index("grid")
    y, z = lax.div(grid, NZ), lax.rem(grid, NZ)
    barrier = pltpu.get_barrier_semaphore()

    def mem_peer(k):
        return {"mem": lax.rem(mem + k, NM)}

    def y_peer(k):
        return {"grid": lax.rem(y + k, NY) * NZ + z}

    def z_peer(k):
        return {"grid": y * NZ + lax.rem(z + k, NZ)}

    for peer, count in ((mem_peer, NM), (y_peer, NY), (z_peer, NZ)):
        for k in range(1, count):
            pl.semaphore_signal(barrier, inc=1, device_id=peer(k), device_id_type=MESH)
    pl.semaphore_wait(barrier, NM + NY + NZ - 3)

    def send(source, target, k, sends, receives, device):
        copy = pltpu.make_async_remote_copy(
            src_ref=source,
            dst_ref=target,
            send_sem=sends.at[k - 1],
            recv_sem=receives.at[k - 1],
            device_id=device,
            device_id_type=MESH,
        )
        copy.start()
        return copy

    def lanes(index):
        return pl.ds(pl.multiple_of(index * 128, 128), 128)

    pending = []
    now = [
        send(src.at[:, lanes(lax.rem(mem + k, NM))], at_m.at[k - 1], k, s1, r1, mem_peer(k))
        for k in range(1, NM)
    ]
    value = src[:, lanes(mem)]
    for k, copy in enumerate(now):
        copy.wait_recv()
        value = value + at_m[k]
    pending += now
    for stage, (peer, count, sends, receives, slots) in enumerate(
        ((y_peer, NY, s2, r2, at_y), (z_peer, NZ, s3, r3, at_z))
    ):
        own[stage] = value
        now = [
            send(own.at[stage], slots.at[k - 1], k, sends, receives, peer(k))
            for k in range(1, count)
        ]
        for k, copy in enumerate(now):
            copy.wait_recv()
            value = value + slots[k]
        pending += now
    own[2] = value
    out[:, lanes(mem)] = value
    now = [
        send(own.at[2], out.at[:, lanes(mem)], k, s4, r4, mem_peer(k)) for k in range(1, NM)
    ]
    for copy in now:
        copy.wait()
    for copy in pending:
        copy.wait_send()


def power_sum(power):
    return pl.pallas_call(
        power_kernel,
        out_shape=jax.ShapeDtypeStruct((8, 1024), f32),
        in_specs=[pl.BlockSpec(memory_space=pltpu.VMEM)],
        out_specs=pl.BlockSpec(memory_space=pltpu.VMEM),
        scratch_shapes=[
            pltpu.VMEM((3, 8, 128), f32),
            pltpu.VMEM((NM - 1, 8, 128), f32),
            pltpu.VMEM((NY - 1, 8, 128), f32),
            pltpu.VMEM((NZ - 1, 8, 128), f32),
        ]
        + [pltpu.SemaphoreType.DMA((n - 1,)) for n in (NM, NM, NY, NY, NZ, NZ, NM, NM)],
        compiler_params=pltpu.CompilerParams(
            collective_id=2, has_side_effects=True, vmem_limit_bytes=BIG
        ),
        name="power_sum",
    )(power)


def synth_kernel(
    power_ref, relax_ref, place_ref, spectral_ref, table_ref, out_a, out_b, ratio, turned
):
    p = pl.program_id(0)

    @pl.when(p == 0)
    def _():
        row = lax.broadcasted_iota(jnp.int32, (TROWS, TROWS), 0)
        column = lax.broadcasted_iota(jnp.int32, (TROWS, TROWS), 1)
        relaxation = jnp.where(
            lax.broadcasted_iota(jnp.int32, (2, TROWS), 0) == 0, relax_ref[0], relax_ref[1]
        )
        place_row = lax.broadcasted_iota(jnp.int32, (2, TROWS), 1)
        odd_row = lax.rem(lax.broadcasted_iota(jnp.int32, (16, TROWS), 0), 2) == 1
        for q in range(2):
            reverse = jnp.where(row + column == 320 - q, 1.0, 0.0).astype(f32)
            part = power_ref[:, q * TROWS : (q + 1) * TROWS]
            flipped = jnp.dot(
                part, reverse, precision=lax.Precision.HIGHEST, preferred_element_type=f32
            )
            power_prior = flipped[0:2] + part[4:6]
            power_post = flipped[2:4] + part[6:8]
            degree = jnp.maximum(2 * place_row + (q - 1), 0).astype(f32)
            samples = MEMBERS * (2.0 * degree + 1.0)
            spread = (power_prior / samples + EPS) / (power_post / samples + EPS)
            value = (1.0 - relaxation) + relaxation * jnp.sqrt(spread)
            back = jnp.dot(
                jnp.concatenate([value] * 4, axis=0),
                reverse,
                precision=lax.Precision.HIGHEST,
                preferred_element_type=f32,
            )
            ratio[q, 0] = jnp.where(odd_row, back[1:2], back[0:1])
            ratio[q, 1] = jnp.where(odd_row, value[1:2], value[0:1])

    pair = place_ref[0] * HALF + p
    odd_pair = lax.rem(p, 2)
    lane = lax.broadcasted_iota(jnp.int32, (16, TROWS), 1)
    for q in range(2):
        in_first = 2 * lane + q < NLAT - pair
        inside = 2 * lane + q <= NLAT
        values = spectral_ref[q]
        rows = jnp.concatenate(
            [
                jnp.where(in_first, values * ratio[q, 0], 0.0),
                jnp.where(inside & ~in_first, values * ratio[q, 1], 0.0),
            ],
            axis=0,
        )
        high, low = split_rows(rows)
        both = jnp.dot(
            jnp.concatenate([high, low], axis=0), table_ref[q], preferred_element_type=f32
        )
        result = both[0:32] + both[32:64]
        a_part = result[:, 0:256] + result[:, 256:512]
        b_part = result[:, 512:640]
        b_part = b_part + pltpu.roll(b_part, 64, 1)
        for e in range(2):
            parity = lax.rem(q + odd_pair + 1 - e, 2)
            for part in range(2):
                at = e * 16 + part * 8 + 4
                start = parity * 160 + p * 4 + e * 2 + part
                where = pl.ds(start, 4, stride=40)
                turned[0, where, :] = a_part[at : at + 4, 0:128]
                turned[1, where, :] = a_part[at : at + 4, 128:256]
                turned[2, where, :] = b_part[at : at + 4]

    @pl.when(p == HALF - 1)
    def _():
        for t in range(2):
            out_a[t * 128 : t * 128 + 128, :] = turned[t].T
        b_rows = turned[2].T
        for g in range(NG):
            out_b[g] = b_rows[g * 2 : g * 2 + 2, :]


def synthesise(power, relaxation, place, spectral, table):
    return pl.pallas_call(
        synth_kernel,
        grid=(HALF,),
        out_shape=(
            jax.ShapeDtypeStruct((NG * 8, TROWS), f32),
            jax.ShapeDtypeStruct((NG, 2, TROWS), f32),
        ),
        in_specs=[
            pl.BlockSpec((8, 1024), lambda i: (0, 0)),
            pl.BlockSpec(memory_space=pltpu.SMEM),
            pl.BlockSpec(memory_space=pltpu.SMEM),
            pl.BlockSpec((2, 16, TROWS), lambda i: (i, 0, 0)),
            pl.BlockSpec((2, TROWS, 640), lambda i: (i, 0, 0)),
        ],
        out_specs=(
            pl.BlockSpec((NG * 8, TROWS), lambda i: (0, 0)),
            pl.BlockSpec((NG, 2, TROWS), lambda i: (0, 0, 0)),
        ),
        scratch_shapes=[
            pltpu.VMEM((2, 2, 16, TROWS), f32),
            pltpu.VMEM((3, TROWS, 128), f32),
        ],
        compiler_params=pltpu.CompilerParams(vmem_limit_bytes=BIG),
        name="synthesise",
    )(power, relaxation, place, spectral, table)


def inverse_kernel(src_a, src_b, mean_ref, high_ref, low_ref, out_ref, split, joined):
    @pl.when(pl.program_id(0) == 0)
    def _():
        for o in range(NG):
            joined[o * 16 : o * 16 + 8, :] = src_a[o * 8 : o * 8 + 8, :]
            joined[o * 16 + 8 : o * 16 + 10, :] = src_b[o]
            joined[o * 16 + 10 : o * 16 + 16, :] = jnp.zeros((6, TROWS), f32)
        for x in range(8):
            row = jnp.concatenate(
                [
                    joined[o * 16 : o * 16 + 16, x * 40 : x * 40 + 40]
                    for o in range(NG)
                ],
                axis=1,
            )
            high, low = split_rows(row)
            split[x * 16 : x * 16 + 16, :] = high
            split[128 + x * 16 : 128 + x * 16 + 16, :] = low

    both = jnp.dot(split[...], high_ref[...], preferred_element_type=f32)
    result = both[0:128] + both[128:256]
    result = result + jnp.dot(split[0:128, :], low_ref[...], preferred_element_type=f32)
    north = result[0:64] + result[64:128]
    south = result[0:64] - result[64:128]
    for h, part in ((0, north), (1, south)):
        for j in range(HALF):
            mean = mean_ref[20 + j * 2 + h]
            for b in range(2):
                for v in range(LEV):
                    row = (b * 2 + v) * 16 + j
                    out_ref[j, h, b, v : v + 1, :] = part[row : row + 1, :] + mean[v : v + 1, :]


def inverse_fourier(returned, mean, high, low):
    width = 640
    return pl.pallas_call(
        inverse_kernel,
        grid=(NLON // width,),
        out_shape=jax.ShapeDtypeStruct((HALF, 2, 2, LEV, NLON), f32),
        in_specs=[
            pl.BlockSpec((NG * 8, TROWS), lambda i: (0, 0)),
            pl.BlockSpec((NG, 2, TROWS), lambda i: (0, 0, 0)),
            pl.BlockSpec((40, LEV, width), lambda i: (0, 0, i)),
            pl.BlockSpec((NLON, width), lambda i: (0, i)),
            pl.BlockSpec((NLON, width), lambda i: (0, i)),
        ],
        out_specs=pl.BlockSpec((HALF, 2, 2, LEV, width), lambda i: (0, 0, 0, 0, i)),
        scratch_shapes=[pltpu.VMEM((256, NLON), bf16), pltpu.VMEM((NG * 16, TROWS), f32)],
        compiler_params=pltpu.CompilerParams(vmem_limit_bytes=BIG),
        name="inverse_fourier",
    )(*returned, mean, high, low)


def lane_order(values):
    grouped = values.reshape(NG, HALF)
    eight = grouped[:, 0:8].reshape(1, 256)
    two = grouped[:, 8:10].reshape(1, 64)
    return jnp.concatenate([eight, two, two], axis=1)


def per_device(prior, posterior, cycle_rows, relaxation):
    forward_high, forward_low, inverse_high, inverse_low = (jnp.asarray(t) for t in trig_tables())
    place = lax.axis_index("grid").astype(jnp.int32)
    place_array = place.reshape(1)
    colatitude = math.pi * (lane_order(cycle_rows).astype(f32) + 0.5) / NLAT
    sines = jnp.sin(colatitude)
    cosines = jnp.cos(colatitude)
    weights = math.pi / NLAT * sines
    pairs = place * HALF + jnp.arange(16, dtype=jnp.int32)
    orders = jnp.clip(jnp.stack([pairs, NLAT - 1 - pairs]), 0, NLAT - 1)
    starts = jnp.take(jnp.asarray(leading_logs()), orders)[:, :, None]
    starts = starts + orders.astype(f32)[:, :, None] * jnp.log(sines)[None]

    mean = member_means(prior, posterior)
    table = legendre_table(starts, cosines, place_array)
    sent = forward_fourier(prior, posterior, mean, forward_high, forward_low)
    arrived = exchange(sent, 1)
    spectral, power = analyse(arrived, weights, place_array, table)
    power = power_sum(power)
    sent_back = synthesise(power, relaxation, place_array, spectral, table)
    returned = exchange(sent_back, 3)
    return inverse_fourier(returned, mean, inverse_high, inverse_low)


def solution(mesh):
    return jax.shard_map(
        per_device,
        mesh=mesh,
        in_specs=(P("grid", None, "mem", None, None), P("grid", None, "mem", None, None), P(), P()),
        out_specs=P("grid", None, "mem", None, None),
        check_vma=False,
    )
```

time: 927 us -> 163 us (0.18); the launches traced: 914 us -> 162 us
  local copies, waits for them, and re-layouts: 304 us -> 2.8 us
  loops' own time: 217 us -> 0 us
  other arithmetic: 213 us -> 2.11 us
  Pallas kernels: 0 us -> 157 us
  blocking collectives: 77.9 us -> 0 us
  matrix products: 52.1 us -> 0 us
  starting transfers between devices: 27.4 us -> 0 us
  between operations: 14.9 us -> 0.07 us
    another operation x2 -> x0, loops' own time: 217 us -> none  [the longest x1 217 us: legendre_table(): lax.scan(advance_two, (empty_state, empty_state, empty_state), jnp.arange...]
    pallas_call x0 -> x9, Pallas kernels: none -> 157 us  [the longest x2 52.1 us: exchange(): pl.pallas_call(exchange_kernel, out_shape=tuple((jax.ShapeDtypeStruct(v.s...]
    slice x85 -> x1, local copies, waits for them, and re-layouts: 83.7 us -> 0.07 us  [lane_order(): two = grouped[:, 8:10].reshape(1, 64)]
    psum x1 -> x0, blocking collectives: 77.9 us -> none  [per_device(): lax.psum((degree_power(spectral_prior, pair_ids, orders, levels), degree_...]
    another operation x650 -> x1, other arithmetic: 73.8 us -> 0.01 us  [per_device(): orders = jnp.clip(jnp.stack([pairs, NLAT - 1 - pairs]), 0, NLAT - 1)]
    reshape x8 -> x1, local copies, waits for them, and re-layouts: 56.9 us -> 0.78 us  [lane_order(): grouped = values.reshape(NG, HALF)]
    dynamic_update_slice x80 -> x0, other arithmetic: 56.1 us -> none  [legendre_table(): lax.scan(advance_two, (empty_state, empty_state, empty_state), jnp.arange...]
    dot_general x6 -> x0, matrix products: 52.1 us -> none  [the longest x2 16.9 us: analyse(): jnp.einsum('ieqn,qewrnc->qeiwrc', legendre, stacked, precision=precise)]
  transfers between devices with their start and end apart: 4 -> 0, of which waited for: 1 -> 0; matrix products, arithmetic and copies ran while one was open for 32% -> 0% of each run, Pallas kernels for 0% -> 0%
where the time goes in v1:
time: 163 us; the launch traced here: 162 us
  Pallas kernels  157 us (96%)
  local copies, waits for them, and re-layouts  2.8 us (2%)
  other arithmetic  2.11 us (1%)
    pallas_call x2, Pallas kernels, exchange(): pl.pallas_call(exchange_kernel, out_shape=tuple((jax.ShapeDtypeStruct(v.s...  52.1 us
    pallas_call x1, Pallas kernels, legendre_table(): pl.pallas_call(legendre_kernel, out_shape=jax.ShapeDtypeStruct((2 * HALF,...  28.7 us
    pallas_call x1, Pallas kernels, power_sum(): pl.pallas_call(power_kernel, out_shape=jax.ShapeDtypeStruct((8, 1024), f3...  21.3 us
    pallas_call x1, Pallas kernels, member_means(): pl.pallas_call(means_kernel, out_shape=jax.ShapeDtypeStruct((40, LEV, NLO...  20 us
    pallas_call x1, Pallas kernels, synthesise(): pl.pallas_call(synth_kernel, grid=(HALF,), out_shape=(jax.ShapeDtypeStruc...  10.7 us
    pallas_call x1, Pallas kernels, analyse(): pl.pallas_call(analyse_kernel, grid=(HALF,), out_shape=(jax.ShapeDtypeStr...  10.5 us
    pallas_call x1, Pallas kernels, forward_fourier(): pl.pallas_call(forward_kernel, grid=(2,), out_shape=(jax.ShapeDtypeStruct...  7.95 us
    pallas_call x1, Pallas kernels, inverse_fourier(): pl.pallas_call(inverse_kernel, grid=(NLON // width,), out_shape=jax.Shape...  6.13 us

profile of v1, /device:TPU:1, one launch (start us, length us, event | category | flops | bytes accessed | tf_op | source)
XLA Modules:
  0.0 162.3 jit_solution(1641892291478231452)
XLA Ops:
  0.0 0.1 reshape.222
  0.1 1.4 gather_fusion
  1.5 0.1 reshape.221
  1.6 0.8 reshape.218
  2.4 0.1 concatenate.48
  2.5 0.1 concatenate.45
  2.6 0.1 slice.11
  2.7 0.1 concatenate.49
  2.8 0.1 concatenate.46
  2.9 0.1 fusion.3
  3.0 0.6 fusion.10
  3.7 0.6 sine_multiply_fusion.weight_ref
  4.3 0.7 multiply_add_fusion.start_ref
  4.9 20.0 %member_means.1.mean_ref = f32[40,2,1280]{2,1,0:T(2,128)} custom-call(f32[10,2,2,2,1280]{4,3,2,1,0:T(2,128)} %prior_ref.3, f32[10,2,2,2,1280]{4,3,2,1,0:T(2,128)} %post_ref.3), custom_call_target="tpu_custom_call" | custom-call | tf_op jit(solution)/shard_map/member_means/pallas_call | solution.py:112
  24.9 8.0 %forward_fourier.1 = (f32[256,640]{1,0:T(8,128)}, f32[32,2,640]{2,1,0:T(2,128)}) custom-call(f32[10,2,2,2,1280]{4,3,2,1,0:T(2,128)} %prior_ref.3, f32[10,2,2,2,1280]{4,3,2,1,0:T(2,128)} %post_ref.3, f32[40,2,1280]{2,1,0:T(2,128)} %member_means.1.mean_ref, bf16[1280,1280]{1,0:T(8,128)(2,1)} %constant.43.clone.high_ref, bf16[1280,1280]{1,0:T(8,128)(2,1)} %constant.44.clone.low_ref), custom_call_target="tpu_custom_call" | custom-call | tf_op jit(solution)/shard_map/forward_fourier/pallas_call | solution.py:270
  32.9 32.5 %exchange_1.1 = (f32[256,640]{1,0:T(8,128)}, f32[32,2,640]{2,1,0:T(2,128)}) custom-call(f32[256,640]{1,0:T(8,128)} %get-tuple-element.15.src_a, f32[32,2,640]{2,1,0:T(2,128)} %get-tuple-element.16.src_b), custom_call_target="tpu_custom_call" | custom-call | tf_op jit(solution)/shard_map/exchange_1/pallas_call | solution.py:337
  65.4 28.7 %legendre_table.1.table_ref = bf16[20,384,640]{2,1,0:T(8,128)(2,1)} custom-call(f32[2,16,384]{2,1,0:T(8,128)} %multiply_add_fusion.start_ref, f32[1,384]{1,0:T(1,128)} %get-tuple-element.25.cosine_ref, s32[1]{0:T(128)} %bitcast.place_ref), custom_call_target="tpu_custom_call" | custom-call | tf_op jit(solution)/shard_map/legendre_table/pallas_call | solution.py:215
  94.1 10.5 %analyse.1 = (f32[20,16,384]{2,1,0:T(8,128)}, f32[8,1024]{1,0:T(8,128)}) custom-call(f32[256,640]{1,0:T(8,128)} %get-tuple-element.17.src_a, f32[32,2,640]{2,1,0:T(2,128)} %get-tuple-element.18.src_b, f32[1,384]{1,0:T(1,128)} %sine_multiply_fusion.weight_ref, s32[1]{0:T(128)} %bitcast.place_ref, bf16[20,384,640]{2,1,0:T(8,128)(2,1)} %legendre_table.1.table_ref), custom_call_target="tpu_custom_call" | custom-call | tf_op jit(solution)/shard_map/analyse/pallas_call | solution.py:418
  104.6 21.3 %power_sum.1.power_ref = f32[8,1024]{1,0:T(8,128)} custom-call(f32[8,1024]{1,0:T(8,128)} %get-tuple-element.19.src), custom_call_target="tpu_custom_call" | custom-call | tf_op jit(solution)/shard_map/power_sum/pallas_call | solution.py:513
  125.9 10.7 %synthesise.1 = (f32[256,384]{1,0:T(8,128)}, f32[32,2,384]{2,1,0:T(2,128)}) custom-call(f32[8,1024]{1,0:T(8,128)} %power_sum.1.power_ref, f32[2]{0:T(128)} %relax_ref.1, s32[1]{0:T(128)} %bitcast.place_ref, f32[20,16,384]{2,1,0:T(8,128)} %get-tuple-element.20.spectral_ref, bf16[20,384,640]{2,1,0:T(8,128)(2,1)} %legendre_table.1.table_ref), custom_call_target="tpu_custom_call" | custom-call | tf_op jit(solution)/shard_map/synthesise/pallas_call | solution.py:609
  136.6 19.6 %exchange_3.1 = (f32[256,384]{1,0:T(8,128)}, f32[32,2,384]{2,1,0:T(2,128)}) custom-call(f32[256,384]{1,0:T(8,128)} %get-tuple-element.21.src_a, f32[32,2,384]{2,1,0:T(2,128)} %get-tuple-element.22.src_b), custom_call_target="tpu_custom_call" | custom-call | tf_op jit(solution)/shard_map/exchange_3/pallas_call | solution.py:337
  156.2 6.1 %inverse_fourier.1 = f32[10,2,2,2,1280]{4,3,2,1,0:T(2,128)} custom-call(f32[256,384]{1,0:T(8,128)} %get-tuple-element.23.src_a, f32[32,2,384]{2,1,0:T(2,128)} %get-tuple-element.24.src_b, f32[40,2,1280]{2,1,0:T(2,128)} %member_means.1.mean_ref, bf16[1280,1280]{1,0:T(8,128)(2,1)} %constant.45.clone.high_ref, bf16[1280,1280]{1,0:T(8,128)(2,1)} %constant.46.clone.low_ref), custom_call_target="tpu_custom_call" | custom-call | tf_op jit(solution)/shard_map/inverse_fourier/pallas_call | solution.py:671
  (6 shorter events, 0.1 us)

commit v2 on v0

v2 whole, which is shorter than its diff:
```python
import functools
import math

import jax
import jax.numpy as jnp
import ml_dtypes
import numpy as np
from jax import lax
from jax.experimental import pallas as pl
from jax.experimental.pallas import tpu as pltpu
from jax.sharding import PartitionSpec as P

MESH = pl.DeviceIdType.MESH
NLAT = 640
LEV = 2
NLON = 1280
NPAIR = 320
MEMBERS = 16
NG = 32
NM = 8
NY = 4
NZ = 8
HALF = 10
EPS = 1e-06
ROWS = 672
TROWS = 384
PITCH = 17
SIDE = 5720
BIG = 60 * 1024 * 1024

f32 = jnp.float32
bf16 = jnp.bfloat16


def split_table(table):
    hi = table.astype(np.float32).astype(ml_dtypes.bfloat16)
    lo = (table - hi.astype(np.float64)).astype(np.float32).astype(ml_dtypes.bfloat16)
    return hi, lo


@functools.lru_cache(maxsize=None)
def trig_tables():
    owner = np.arange(NG)[:, None, None]
    pair = np.arange(HALF)[None, :, None]
    segment = np.arange(2)[None, None, :]
    first = owner * HALF + pair
    order = np.where(segment == 0, first, NLAT - 1 - first).reshape(-1)
    phase = (np.arange(NLON)[:, None] * order[None, :]) % NLON
    angle = 2.0 * np.pi / NLON * phase
    table = np.stack([np.cos(angle), -np.sin(angle)], axis=-1).reshape(NLON, NLON)
    weight = np.repeat(np.where(order == 0, 1.0, 2.0) / NLON, 2)
    return split_table(table) + split_table((table * weight[None, :]).T)


@functools.lru_cache(maxsize=None)
def leading_logs():
    i = np.arange(1, NLAT + 1, dtype=np.float64)
    total = np.concatenate([[0.0], np.cumsum(np.log((2 * i - 1) / (2 * i)))])[:NLAT]
    m = np.arange(NLAT, dtype=np.float64)
    leading = 0.5 * (np.log((2 * m + 1) / 2) + total)
    pair = np.arange(NG)[:, None] * HALF + np.arange(16)[None, :]
    orders = np.clip(np.stack([pair, NLAT - 1 - pair], axis=1), 0, NLAT - 1)
    return np.ascontiguousarray(
        np.broadcast_to(leading[orders][..., None], (NG, 2, 16, 128)).astype(np.float32)
    )


def split_rows(values):
    high = values.astype(bf16)
    low = (values - high.astype(f32)).astype(bf16)
    return high, low


def place_of(side, index):
    return side * SIDE + index * PITCH


def build_legendre(place, lead_ref, lats_ref, table_ref, rows):
    zero = jnp.zeros((16, TROWS), f32)
    for i in range(641, ROWS):
        for t in range(3):
            rows[t, pl.ds(place_of(i % 2, i // 2), 16), :] = zero[:, 0:128]
    sub = lax.broadcasted_iota(jnp.int32, (16, 128), 0)
    step = lax.rem(lax.broadcasted_iota(jnp.int32, (16, 128), 1), 8)
    cosine = jnp.broadcast_to(lats_ref[0:1, :], (16, TROWS))
    log_sine = jnp.broadcast_to(lats_ref[2:3, :], (16, TROWS))
    valid = sub < HALF
    pair = jnp.where(valid, place * HALF + sub, 4 * NLAT)

    def chain(segment, first_block, order):
        def block(b, state):
            current, earlier, scale_log = state
            degree = (b * 8 + step).astype(f32)
            m = order.astype(f32)
            inside = valid & (b * 8 + step > order)
            square = degree * degree
            difference = jnp.where(inside, square - m * m, 1.0)
            low = degree - 1.0
            low_square = low * low
            lead = (4.0 * square - 1.0) / difference
            trail = jnp.maximum(low_square - m * m, 0.0) / jnp.maximum(4.0 * low_square - 1.0, 1.0)
            a = jnp.where(inside, jnp.sqrt(jnp.maximum(lead, 0.0)), 0.0)
            c = jnp.where(inside, a * jnp.sqrt(trail), 0.0)
            scale = jnp.exp(scale_log)
            for k in range(8):
                ak = jnp.broadcast_to(a[:, k : k + 1], (16, TROWS))
                ck = jnp.broadcast_to(c[:, k : k + 1], (16, TROWS))
                following = (ak * cosine) * current - ck * earlier
                begin = order == b * 8 + k
                following = jnp.where(jnp.concatenate([begin] * 3, axis=1), 1.0, following)
                earlier = current
                current = following
                entry = current * scale
                degree_now = b * 8 + k
                side = (k + 1) % 2
                if segment == 0:
                    offset = place_of(side, (NLAT - 1 - k - side) // 2 - 4 * b)
                else:
                    offset = place_of(side, 4 * b + (k + 1 - side) // 2)
                    second = degree_now >= NLAT - 1 - pair
                for t in range(3):
                    tile = entry[:, t * 128 : t * 128 + 128]
                    if segment == 1:
                        tile = jnp.where(second, tile, rows[t, pl.ds(offset, 16), :])
                    rows[t, pl.ds(offset, 16), :] = tile
            large = jnp.abs(current) > 1e10
            current = jnp.where(large, current * 1e-20, current)
            earlier = jnp.where(large, earlier * 1e-20, earlier)
            scale_log = jnp.where(large, scale_log + 20.0 * math.log(10.0), scale_log)
            return current, earlier, scale_log

        leading = jnp.concatenate([lead_ref[segment]] * 3, axis=1)
        wide = jnp.concatenate([order.astype(f32)] * 3, axis=1)
        lax.fori_loop(first_block, NLAT // 8, block, (zero, zero, leading + wide * log_sine))

    chain(0, lax.div(place * HALF, 8), pair)
    chain(1, lax.div(NLAT - HALF - place * HALF, 8), NLAT - 1 - pair)

    right = lax.broadcasted_iota(jnp.int32, (16, 128), 1) < 64
    blank = jnp.zeros((TROWS - ROWS // 2, 640), bf16)
    for p in range(HALF):
        for q in range(2):

            def convert(t, carry):
                out = pl.ds(pl.multiple_of(t * 16, 16), 16)
                for tile in range(3):
                    values = rows[tile, pl.ds(q * SIDE + t * 16 * PITCH + p, 16, stride=PITCH), :]
                    high = values.astype(bf16)
                    low = values - high.astype(f32)
                    if tile < 2:
                        at = tile * 128
                        table_ref[p * 2 + q, out, at : at + 128] = high
                        table_ref[p * 2 + q, out, at + 256 : at + 384] = low.astype(bf16)
                    else:
                        table_ref[p * 2 + q, out, 512:640] = jnp.where(right, values, low).astype(bf16)
                return carry

            lax.fori_loop(0, ROWS // 32, convert, 0, unroll=3)
            table_ref[p * 2 + q, ROWS // 2 : TROWS, :] = blank


def spectral_kernel(
    prior_ref,
    post_ref,
    lats_ref,
    relax_ref,
    lead_hbm,
    high_hbm,
    low_hbm,
    mean_ref,
    back_a,
    back_b,
    sums,
    arrived,
    piece,
    lead,
    trig_high,
    trig_low,
    left,
    split,
    out_a,
    out_b,
    in_a,
    in_b,
    rows,
    table,
    pairs,
    turned,
    total,
    spectral,
    power,
    summed,
    own,
    at_m,
    at_y,
    at_z,
    ratio,
    merged,
    ret_a,
    ret_b,
    local_sem,
    s_rs,
    r_rs,
    s_ag,
    r_ag,
    s_ex,
    r_ex,
    s_p1,
    r_p1,
    s_p2,
    r_p2,
    s_p3,
    r_p3,
    s_p4,
    r_p4,
    s_re,
    r_re,
):
    mem = lax.axis_index("mem")
    me = lax.axis_index("grid")
    y, z = lax.div(me, NZ), lax.rem(me, NZ)
    barrier = pltpu.get_barrier_semaphore()

    def peer_of(k):
        return lax.rem(y + k // NZ, NY) * NZ + lax.rem(z + k % NZ, NZ)

    def eight(place):
        return pl.ds(pl.multiple_of(place * 8, 8), 8)

    def mem_peer(k):
        return {"mem": lax.rem(mem + k, NM)}

    def send(source, target, send_sem, recv_sem, device):
        copy = pltpu.make_async_remote_copy(
            src_ref=source,
            dst_ref=target,
            send_sem=send_sem,
            recv_sem=recv_sem,
            device_id=device,
            device_id_type=MESH,
        )
        copy.start()
        return copy

    for k in range(1, NM):
        pl.semaphore_signal(barrier, inc=1, device_id=mem_peer(k), device_id_type=MESH)
    for k in range(1, NG):
        pl.semaphore_signal(barrier, inc=1, device_id={"grid": peer_of(k)}, device_id_type=MESH)
    loads = [
        pltpu.make_async_copy(high_hbm, trig_high, local_sem.at[0]),
        pltpu.make_async_copy(low_hbm, trig_low, local_sem.at[1]),
        pltpu.make_async_copy(lead_hbm.at[me], lead, local_sem.at[2]),
    ]
    for copy in loads:
        copy.start()

    for ens, ref in ((0, prior_ref), (1, post_ref)):
        for j in range(HALF):
            for h in range(2):
                sums[ens * 20 + j * 2 + h] = ref[j, h, 0] + ref[j, h, 1]
    left[...] = jnp.zeros_like(left)
    pl.semaphore_wait(barrier, NM + NG - 2)
    pending = []
    now = []
    for k in range(1, NM):
        peer = lax.rem(mem + k, NM)
        now.append(
            send(
                sums.at[pl.ds(peer * 5, 5)],
                arrived.at[k - 1],
                s_rs.at[k - 1],
                r_rs.at[k - 1],
                mem_peer(k),
            )
        )
    value = sums[pl.ds(mem * 5, 5)]
    for k, copy in enumerate(now):
        copy.wait_recv()
        value = value + arrived[k]
    pending += now
    piece[...] = value * (1.0 / MEMBERS)
    mean_ref[pl.ds(mem * 5, 5)] = piece[...]
    now = [
        send(piece, mean_ref.at[pl.ds(mem * 5, 5)], s_ag.at[k - 1], r_ag.at[k - 1], mem_peer(k))
        for k in range(1, NM)
    ]
    for copy in now:
        copy.wait_recv()
    pending += now

    for ens, ref in ((0, prior_ref), (1, post_ref)):
        for j in range(HALF):
            north_mean = mean_ref[ens * 20 + j * 2]
            south_mean = mean_ref[ens * 20 + j * 2 + 1]
            for b in range(2):
                north = ref[j, 0, b] - north_mean
                south = ref[j, 1, b] - south_mean
                for q, part in ((0, north + south), (1, north - south)):
                    for v in range(LEV):
                        row = (q * 8 + ens * 4 + b * 2 + v) * 16 + j
                        left[row : row + 1, :] = part[v : v + 1, :]
    high, low = split_rows(left[...])
    split[0:256, :] = high
    split[256:512, :] = low
    for copy in loads:
        copy.wait()
    own_half = lax.div(y, 2)
    exchanged = []
    for step in range(2):
        half = own_half if step == 0 else 1 - own_half
        columns = pl.ds(pl.multiple_of(half * 640, 128), 640)
        both = jnp.dot(split[...], trig_high[:, columns], preferred_element_type=f32)
        result = both[0:256] + both[256:512]
        result = result + jnp.dot(
            split[0:256, :], trig_low[:, columns], preferred_element_type=f32
        )
        for o in range(16):
            block = jnp.concatenate(
                [result[x * 16 : x * 16 + 16, o * 40 : o * 40 + 40] for x in range(16)], axis=1
            )
            place = half * 16 + o
            out_a[eight(place), :] = block[0:8]
            out_b[place] = block[8:10]
        for j in range(2):
            if step == 0:
                far_y = y if j == 0 else y + 1 - 2 * lax.rem(y, 2)
            else:
                far_y = 2 * half + lax.rem(y + j, 2)
            for dz in (4, 3, 5, 2, 6, 1, 7, 0):
                if step == 0 and j == 0 and dz == 0:
                    continue
                peer = far_y * NZ + lax.rem(z + dz, NZ)
                k = (step * 2 + j) * 8 + dz
                exchanged.append(
                    send(
                        out_a.at[eight(peer), :],
                        in_a.at[eight(me), :],
                        s_ex.at[0, k],
                        r_ex.at[0, k],
                        {"grid": peer},
                    )
                )
                exchanged.append(
                    send(out_b.at[peer], in_b.at[me], s_ex.at[1, k], r_ex.at[1, k], {"grid": peer})
                )

    build_legendre(me, lead, lats_ref, table, rows)

    in_a[eight(me), :] = out_a[eight(me), :]
    in_b[me] = out_b[me]
    for copy in exchanged:
        copy.wait_recv()
    pending += exchanged
    for g in range(NG):
        two = in_b[g]
        pairs[g * 2 : g * 2 + 2, :] = two
        pairs[64 + g * 2 : 64 + g * 2 + 2, :] = two
    for t in range(2):
        at = t * 128
        turned[t] = in_a[at : at + 128, :].T * lats_ref[1:2, at : at + 128]
    turned[2] = pairs[...].T * lats_ref[1:2, 256:384]
    total[...] = jnp.zeros_like(total)
    lane = lax.broadcasted_iota(jnp.int32, (16, TROWS), 1)

    def analyse_pair(p, odd):
        pair = me * HALF + p
        first_weight = jnp.where(pair == 0, 1.0, 2.0).astype(f32)
        for q in range(2):
            groups = []
            for e in range(2):
                parity = (q + odd + 1 - e) % 2
                for part in range(2):
                    start = parity * 320 + p * 4 + e * 2 + part
                    groups.append(
                        jnp.concatenate(
                            [turned[t, pl.ds(start, 8, stride=40), :] for t in range(3)], axis=1
                        )
                    )
            high, low = split_rows(jnp.concatenate(groups, axis=0))
            operand = jnp.concatenate(
                [
                    jnp.concatenate([high[:, 0:256], high[:, 0:256], high[:, 256:384]], axis=1),
                    jnp.concatenate([low[:, 0:256], low[:, 0:256], low[:, 256:384]], axis=1),
                ],
                axis=0,
            )
            both = lax.dot_general(
                operand,
                table[p * 2 + q],
                (((1,), (1,)), ((), ())),
                preferred_element_type=f32,
            )
            result = both[0:32] + both[32:64]
            in_first = 2 * lane + q < NLAT - pair
            chosen = jnp.where(in_first, result[0:16], result[16:32])
            spectral[p * 2 + q] = chosen
            squares = chosen * chosen
            where = slice(q * TROWS, (q + 1) * TROWS)
            total[0, :, where] += jnp.where(in_first, squares, 0.0) * first_weight
            total[1, :, where] += jnp.where(in_first, 0.0, squares) * 2.0

    def analyse_two(i, carry):
        analyse_pair(2 * i, 0)
        analyse_pair(2 * i + 1, 1)
        return carry

    lax.fori_loop(0, HALF // 2, analyse_two, 0)
    for s in range(2):
        both = total[s, 0:8, :] + total[s, 8:16, :]
        for ens in range(2):
            row = s * 4 + ens * 2
            power[row : row + 2, 0:768] = both[ens * 4 : ens * 4 + 2] + both[ens * 4 + 2 : ens * 4 + 4]
    power[:, 768:1024] = jnp.zeros((8, 256), f32)

    def lanes(index):
        return pl.ds(pl.multiple_of(index * 128, 128), 128)

    now = [
        send(
            power.at[:, lanes(lax.rem(mem + k, NM))],
            at_m.at[k - 1],
            s_p1.at[k - 1],
            r_p1.at[k - 1],
            mem_peer(k),
        )
        for k in range(1, NM)
    ]
    value = power[:, lanes(mem)]
    for k, copy in enumerate(now):
        copy.wait_recv()
        value = value + at_m[k]
    pending += now

    def y_peer(k):
        return {"grid": lax.rem(y + k, NY) * NZ + z}

    def z_peer(k):
        return {"grid": y * NZ + lax.rem(z + k, NZ)}

    for stage, (peer, count, sends, receives, slots) in enumerate(
        ((y_peer, NY, s_p2, r_p2, at_y), (z_peer, NZ, s_p3, r_p3, at_z))
    ):
        own[stage] = value
        now = [
            send(own.at[stage], slots.at[k - 1], sends.at[k - 1], receives.at[k - 1], peer(k))
            for k in range(1, count)
        ]
        for k, copy in enumerate(now):
            copy.wait_recv()
            value = value + slots[k]
        pending += now
    own[2] = value
    summed[:, lanes(mem)] = value
    now = [
        send(own.at[2], summed.at[:, lanes(mem)], s_p4.at[k - 1], r_p4.at[k - 1], mem_peer(k))
        for k in range(1, NM)
    ]
    for copy in now:
        copy.wait_recv()
    pending += now

    row = lax.broadcasted_iota(jnp.int32, (TROWS, TROWS), 0)
    column = lax.broadcasted_iota(jnp.int32, (TROWS, TROWS), 1)
    relaxation = jnp.where(
        lax.broadcasted_iota(jnp.int32, (2, TROWS), 0) == 0, relax_ref[0], relax_ref[1]
    )
    place_row = lax.broadcasted_iota(jnp.int32, (2, TROWS), 1)
    odd_row = lax.rem(lax.broadcasted_iota(jnp.int32, (16, TROWS), 0), 2) == 1
    for q in range(2):
        reverse = jnp.where(row + column == 320 - q, 1.0, 0.0).astype(f32)
        part = summed[:, q * TROWS : (q + 1) * TROWS]
        flipped = jnp.dot(
            part, reverse, precision=lax.Precision.HIGHEST, preferred_element_type=f32
        )
        power_prior = flipped[0:2] + part[4:6]
        power_post = flipped[2:4] + part[6:8]
        degree = jnp.maximum(2 * place_row + (q - 1), 0).astype(f32)
        samples = MEMBERS * (2.0 * degree + 1.0)
        spread = (power_prior / samples + EPS) / (power_post / samples + EPS)
        value = (1.0 - relaxation) + relaxation * jnp.sqrt(spread)
        back = jnp.dot(
            jnp.concatenate([value] * 4, axis=0),
            reverse,
            precision=lax.Precision.HIGHEST,
            preferred_element_type=f32,
        )
        ratio[q, 0] = jnp.where(odd_row, back[1:2], back[0:1])
        ratio[q, 1] = jnp.where(odd_row, value[1:2], value[0:1])

    def synth_pair(p, odd):
        pair = me * HALF + p
        for q in range(2):
            in_first = 2 * lane + q < NLAT - pair
            inside = 2 * lane + q <= NLAT
            values = spectral[p * 2 + q]
            high, low = split_rows(
                jnp.concatenate(
                    [
                        jnp.where(in_first, values * ratio[q, 0], 0.0),
                        jnp.where(inside & ~in_first, values * ratio[q, 1], 0.0),
                    ],
                    axis=0,
                )
            )
            both = jnp.dot(
                jnp.concatenate([high, low], axis=0),
                table[p * 2 + q],
                preferred_element_type=f32,
            )
            result = both[0:32] + both[32:64]
            a_part = result[:, 0:256] + result[:, 256:512]
            b_part = result[:, 512:640]
            b_part = b_part + pltpu.roll(b_part, 64, 1)
            for e in range(2):
                parity = (q + odd + 1 - e) % 2
                for part in range(2):
                    at = e * 16 + part * 8 + 4
                    start = parity * 160 + p * 4 + e * 2 + part
                    where = pl.ds(start, 4, stride=40)
                    merged[0, where, :] = a_part[at : at + 4, 0:128]
                    merged[1, where, :] = a_part[at : at + 4, 128:256]
                    merged[2, where, :] = b_part[at : at + 4]

    def synth_two(i, carry):
        synth_pair(2 * i, 0)
        synth_pair(2 * i + 1, 1)
        return carry

    merged[:, 320:384, :] = jnp.zeros((3, 64, 128), f32)
    lax.fori_loop(0, HALF // 2, synth_two, 0)
    for t in range(2):
        ret_a[t * 128 : t * 128 + 128, :] = merged[t].T
    b_rows = merged[2].T
    for g in range(NG):
        ret_b[g] = b_rows[g * 2 : g * 2 + 2, :]

    now = []
    for k in sorted(range(1, NG), key=lambda k: -min(k % NZ, NZ - k % NZ)):
        peer = peer_of(k)
        now.append(
            send(
                ret_a.at[eight(peer), :],
                back_a.at[eight(me), :],
                s_re.at[0, k],
                r_re.at[0, k],
                {"grid": peer},
            )
        )
        now.append(
            send(ret_b.at[peer], back_b.at[me], s_re.at[1, k], r_re.at[1, k], {"grid": peer})
        )
    back_a[eight(me), :] = ret_a[eight(me), :]
    back_b[me] = ret_b[me]
    for copy in now:
        copy.wait()
    for copy in pending:
        copy.wait_send()


def spectral(prior, posterior, lats, relaxation, lead, high, low):
    vmem = pl.BlockSpec(memory_space=pltpu.VMEM)
    hbm = pl.BlockSpec(memory_space=pl.ANY)
    return pl.pallas_call(
        spectral_kernel,
        out_shape=(
            jax.ShapeDtypeStruct((40, LEV, NLON), f32),
            jax.ShapeDtypeStruct((NG * 8, TROWS), f32),
            jax.ShapeDtypeStruct((NG, 2, TROWS), f32),
        ),
        in_specs=[vmem, vmem, vmem, pl.BlockSpec(memory_space=pltpu.SMEM), hbm, hbm, hbm],
        out_specs=(vmem, vmem, vmem),
        scratch_shapes=[
            pltpu.VMEM((40, LEV, NLON), f32),
            pltpu.VMEM((NM - 1, 5, LEV, NLON), f32),
            pltpu.VMEM((5, LEV, NLON), f32),
            pltpu.VMEM((2, 16, 128), f32),
            pltpu.VMEM((NLON, NLON), bf16),
            pltpu.VMEM((NLON, NLON), bf16),
            pltpu.VMEM((256, NLON), f32),
            pltpu.VMEM((512, NLON), bf16),
            pltpu.VMEM((NG * 8, 640), f32),
            pltpu.VMEM((NG, 2, 640), f32),
            pltpu.VMEM((NG * 8, 640), f32),
            pltpu.VMEM((NG, 2, 640), f32),
            pltpu.VMEM((3, 2 * SIDE, 128), f32),
            pltpu.VMEM((2 * HALF, TROWS, 640), bf16),
            pltpu.VMEM((128, 640), f32),
            pltpu.VMEM((3, 640, 128), f32),
            pltpu.VMEM((2, 16, 2 * TROWS), f32),
            pltpu.VMEM((2 * HALF, 16, TROWS), f32),
            pltpu.VMEM((8, 1024), f32),
            pltpu.VMEM((8, 1024), f32),
            pltpu.VMEM((3, 8, 128), f32),
            pltpu.VMEM((NM - 1, 8, 128), f32),
            pltpu.VMEM((NY - 1, 8, 128), f32),
            pltpu.VMEM((NZ - 1, 8, 128), f32),
            pltpu.VMEM((2, 2, 16, TROWS), f32),
            pltpu.VMEM((3, TROWS, 128), f32),
            pltpu.VMEM((NG * 8, TROWS), f32),
            pltpu.VMEM((NG, 2, TROWS), f32),
            pltpu.SemaphoreType.DMA((3,)),
        ]
        + [pltpu.SemaphoreType.DMA((NM - 1,)) for _ in range(4)]
        + [pltpu.SemaphoreType.DMA((2, NG)) for _ in range(2)]
        + [pltpu.SemaphoreType.DMA((n - 1,)) for n in (NM, NM, NY, NY, NZ, NZ, NM, NM)]
        + [pltpu.SemaphoreType.DMA((2, NG)) for _ in range(2)],
        compiler_params=pltpu.CompilerParams(
            collective_id=0, has_side_effects=True, vmem_limit_bytes=BIG
        ),
        name="spectral",
    )(prior, posterior, lats, relaxation, lead, high, low)


def inverse_kernel(src_a, src_b, mean_ref, high_ref, low_ref, out_ref, split, joined):
    @pl.when(pl.program_id(0) == 0)
    def _():
        for o in range(NG):
            joined[o * 16 : o * 16 + 8, :] = src_a[o * 8 : o * 8 + 8, :]
            joined[o * 16 + 8 : o * 16 + 10, :] = src_b[o]
            joined[o * 16 + 10 : o * 16 + 16, :] = jnp.zeros((6, TROWS), f32)
        for x in range(8):
            row = jnp.concatenate(
                [
                    joined[o * 16 : o * 16 + 16, x * 40 : x * 40 + 40]
                    for o in range(NG)
                ],
                axis=1,
            )
            high, low = split_rows(row)
            split[x * 16 : x * 16 + 16, :] = high
            split[128 + x * 16 : 128 + x * 16 + 16, :] = low

    both = jnp.dot(split[...], high_ref[...], preferred_element_type=f32)
    result = both[0:128] + both[128:256]
    result = result + jnp.dot(split[0:128, :], low_ref[...], preferred_element_type=f32)
    north = result[0:64] + result[64:128]
    south = result[0:64] - result[64:128]
    for h, part in ((0, north), (1, south)):
        for j in range(HALF):
            mean = mean_ref[20 + j * 2 + h]
            for b in range(2):
                for v in range(LEV):
                    row = (b * 2 + v) * 16 + j
                    out_ref[j, h, b, v : v + 1, :] = part[row : row + 1, :] + mean[v : v + 1, :]


def inverse_fourier(returned, mean, high, low):
    width = 640
    return pl.pallas_call(
        inverse_kernel,
        grid=(NLON // width,),
        out_shape=jax.ShapeDtypeStruct((HALF, 2, 2, LEV, NLON), f32),
        in_specs=[
            pl.BlockSpec((NG * 8, TROWS), lambda i: (0, 0)),
            pl.BlockSpec((NG, 2, TROWS), lambda i: (0, 0, 0)),
            pl.BlockSpec((40, LEV, width), lambda i: (0, 0, i)),
            pl.BlockSpec((NLON, width), lambda i: (0, i)),
            pl.BlockSpec((NLON, width), lambda i: (0, i)),
        ],
        out_specs=pl.BlockSpec((HALF, 2, 2, LEV, width), lambda i: (0, 0, 0, 0, i)),
        scratch_shapes=[pltpu.VMEM((256, NLON), bf16), pltpu.VMEM((NG * 16, TROWS), f32)],
        compiler_params=pltpu.CompilerParams(vmem_limit_bytes=BIG),
        name="inverse_fourier",
    )(*returned, mean, high, low)


def lane_order():
    grouped = np.arange(NPAIR).reshape(NG, HALF)
    two = grouped[:, 8:10].reshape(-1)
    return np.concatenate([grouped[:, 0:8].reshape(-1), two, two]).astype(np.int32)


def per_device(prior, posterior, cycle_rows, relaxation):
    forward_high, forward_low, inverse_high, inverse_low = (jnp.asarray(t) for t in trig_tables())
    rows = jnp.take(cycle_rows, jnp.asarray(lane_order()))
    colatitude = math.pi * (rows.astype(f32) + 0.5) / NLAT
    sines = jnp.sin(colatitude)
    lats = jnp.stack([jnp.cos(colatitude), math.pi / NLAT * sines, jnp.log(sines)])
    mean, back_a, back_b = spectral(
        prior, posterior, lats, relaxation, jnp.asarray(leading_logs()), forward_high, forward_low
    )
    return inverse_fourier((back_a, back_b), mean, inverse_high, inverse_low)


def solution(mesh):
    return jax.shard_map(
        per_device,
        mesh=mesh,
        in_specs=(P("grid", None, "mem", None, None), P("grid", None, "mem", None, None), P(), P()),
        out_specs=P("grid", None, "mem", None, None),
        check_vma=False,
    )
```

time: 927 us -> 101 us (0.11); the launches traced: 914 us -> 100 us
  local copies, waits for them, and re-layouts: 304 us -> 2.8 us
  loops' own time: 217 us -> 0 us
  other arithmetic: 213 us -> 1.35 us
  Pallas kernels: 0 us -> 96.2 us
  blocking collectives: 77.9 us -> 0 us
  matrix products: 52.1 us -> 0 us
  starting transfers between devices: 27.4 us -> 0 us
  between operations: 14.9 us -> 0.04 us
    another operation x2 -> x0, loops' own time: 217 us -> none  [the longest x1 217 us: legendre_table(): lax.scan(advance_two, (empty_state, empty_state, empty_state), jnp.arange...]
    pallas_call x0 -> x2, Pallas kernels: none -> 96.2 us  [the longest x1 90.1 us: spectral(): pl.pallas_call(spectral_kernel, out_shape=(jax.ShapeDtypeStruct((40, LEV,...]
    slice x85 -> x0, local copies, waits for them, and re-layouts: 83.7 us -> none  [the longest x81 54.1 us: legendre_table(): lax.scan(advance_two, (empty_state, empty_state, empty_state), jnp.arange...]
    psum x1 -> x0, blocking collectives: 77.9 us -> none  [per_device(): lax.psum((degree_power(spectral_prior, pair_ids, orders, levels), degree_...]
    another operation x650 -> x1, other arithmetic: 73.8 us -> 0.6 us  [per_device(): jnp.stack([jnp.cos(colatitude), math.pi / NLAT * sines, jnp.log(sines)])]
    reshape x8 -> x0, local copies, waits for them, and re-layouts: 56.9 us -> none  [the longest x2 23.7 us: to_slots(): arrived.reshape(2 * half_slots, 2, grid_count * cycle_pairs, halves, colu...]
    dynamic_update_slice x80 -> x0, other arithmetic: 56.1 us -> none  [legendre_table(): lax.scan(advance_two, (empty_state, empty_state, empty_state), jnp.arange...]
    dot_general x6 -> x0, matrix products: 52.1 us -> none  [the longest x2 16.9 us: analyse(): jnp.einsum('ieqn,qewrnc->qeiwrc', legendre, stacked, precision=precise)]
  transfers between devices with their start and end apart: 4 -> 0, of which waited for: 1 -> 0; matrix products, arithmetic and copies ran while one was open for 32% -> 0% of each run, Pallas kernels for 0% -> 0%
where the time goes in v2:
time: 101 us; the launch traced here: 100 us
  Pallas kernels  96.2 us (95%)
  local copies, waits for them, and re-layouts  2.8 us (3%)
  other arithmetic  1.35 us (1%)
    pallas_call x1, Pallas kernels, spectral(): pl.pallas_call(spectral_kernel, out_shape=(jax.ShapeDtypeStruct((40, LEV,...  90.1 us
    pallas_call x1, Pallas kernels, inverse_fourier(): pl.pallas_call(inverse_kernel, grid=(NLON // width,), out_shape=jax.Shape...  6.13 us
    gather x1, local copies, waits for them, and re-layouts, per_device(): rows = jnp.take(cycle_rows, jnp.asarray(lane_order()))  2.79 us

profile of v2, /device:TPU:1, one launch (start us, length us, event | category | flops | bytes accessed | tf_op | source)
XLA Modules:
  0.0 100.4 jit_solution(277004383710641735)
XLA Ops:
  0.0 0.0 copy-start
  0.0 0.7 pad_clamp_fusion
  0.7 0.0 copy-done
  0.7 2.8 %gather_fusion = s32[384]{0:T(512)S(1)} fusion(s32[320]{0:T(512)S(1)} %copy-done, s32[1024]{0:T(1024)S(1)} %pad_clamp_fusion), kind=kCustom, calls=%fused_computation | custom fusion | bytes 4608 | tf_op jit(solution)/shard_map/jit(_take)/gather | solution.py:675
  3.6 0.6 pad_maximum_fusion.lats_ref
  4.2 90.1 %spectral.1 = (f32[40,2,1280]{2,1,0:T(2,128)}, f32[256,384]{1,0:T(8,128)}, f32[32,2,384]{2,1,0:T(2,128)}) custom-call(f32[10,2,2,2,1280]{4,3,2,1,0:T(2,128)} %prior_ref.1, f32[10,2,2,2,1280]{4,3,2,1,0:T(2,128)} %post_ref.1, f32[3,384]{1,0:T(4,128)} %pad_maximum_fusion.lats_ref, f32[2]{0:T(128)} %relax_ref.1, f32[32,2,16,128]{3,2,1,0:T(8,128)} %constant.41.clone.lead_hbm, ...), custom_call_target="tpu_custom_call" | custom-call | tf_op jit(solution)/shard_map/spectral/pallas_call | solution.py:563
  94.3 6.1 %inverse_fourier.1 = f32[10,2,2,2,1280]{4,3,2,1,0:T(2,128)} custom-call(f32[256,384]{1,0:T(8,128)} %get-tuple-element.8.src_a, f32[32,2,384]{2,1,0:T(2,128)} %get-tuple-element.9.src_b, f32[40,2,1280]{2,1,0:T(2,128)} %get-tuple-element.10.mean_ref, bf16[1280,1280]{1,0:T(8,128)(2,1)} %constant.38.clone.high_ref, bf16[1280,1280]{1,0:T(8,128)(2,1)} %constant.39.clone.low_ref), custom_call_target="tpu_custom_call" | custom-call | tf_op jit(solution)/shard_map/inverse_fourier/pallas_call | solution.py:649
  (4 shorter events, 0.1 us)
Async XLA Ops:
  0.0 0.7 copy-start

commit v3 on v2

--- a/solution.py
+++ b/solution.py
@@ -25,6 +25,7 @@
 ROWS = 672
 TROWS = 384
 PITCH = 17
+EARLY = 32
 SIDE = 5720
 BIG = 60 * 1024 * 1024
 
@@ -75,11 +76,8 @@
     return side * SIDE + index * PITCH
 
 
-def build_legendre(place, lead_ref, lats_ref, table_ref, rows):
+def legendre_parts(place, lead_ref, lats_ref, table_ref, rows, early):
     zero = jnp.zeros((16, TROWS), f32)
-    for i in range(641, ROWS):
-        for t in range(3):
-            rows[t, pl.ds(place_of(i % 2, i // 2), 16), :] = zero[:, 0:128]
     sub = lax.broadcasted_iota(jnp.int32, (16, 128), 0)
     step = lax.rem(lax.broadcasted_iota(jnp.int32, (16, 128), 1), 8)
     cosine = jnp.broadcast_to(lats_ref[0:1, :], (16, TROWS))
@@ -87,7 +85,7 @@
     valid = sub < HALF
     pair = jnp.where(valid, place * HALF + sub, 4 * NLAT)
 
-    def chain(segment, first_block, order):
+    def chain(segment, first_block, last_block, order, state=None):
         def block(b, state):
             current, earlier, scale_log = state
             degree = (b * 8 + step).astype(f32)
@@ -131,38 +129,52 @@
 
         leading = jnp.concatenate([lead_ref[segment]] * 3, axis=1)
         wide = jnp.concatenate([order.astype(f32)] * 3, axis=1)
-        lax.fori_loop(first_block, NLAT // 8, block, (zero, zero, leading + wide * log_sine))
-
-    chain(0, lax.div(place * HALF, 8), pair)
-    chain(1, lax.div(NLAT - HALF - place * HALF, 8), NLAT - 1 - pair)
-
-    right = lax.broadcasted_iota(jnp.int32, (16, 128), 1) < 64
-    blank = jnp.zeros((TROWS - ROWS // 2, 640), bf16)
-    for p in range(HALF):
-        for q in range(2):
-
-            def convert(t, carry):
-                out = pl.ds(pl.multiple_of(t * 16, 16), 16)
-                for tile in range(3):
-                    values = rows[tile, pl.ds(q * SIDE + t * 16 * PITCH + p, 16, stride=PITCH), :]
-                    high = values.astype(bf16)
-                    low = values - high.astype(f32)
-                    if tile < 2:
-                        at = tile * 128
-                        table_ref[p * 2 + q, out, at : at + 128] = high
-                        table_ref[p * 2 + q, out, at + 256 : at + 384] = low.astype(bf16)
-                    else:
-                        table_ref[p * 2 + q, out, 512:640] = jnp.where(right, values, low).astype(bf16)
-                return carry
-
-            lax.fori_loop(0, ROWS // 32, convert, 0, unroll=3)
-            table_ref[p * 2 + q, ROWS // 2 : TROWS, :] = blank
+        if state is None:
+            state = (zero, zero, leading + wide * log_sine)
+        return lax.fori_loop(first_block, last_block, block, state)
+
+    begin_block = lax.div(place * HALF, 8)
+    middle = jnp.minimum(begin_block + early, NLAT // 8)
+
+    def start():
+        for i in range(641, ROWS):
+            for t in range(3):
+                rows[t, pl.ds(place_of(i % 2, i // 2), 16), :] = zero[:, 0:128]
+        return chain(0, begin_block, middle, pair)
+
+    def finish(state):
+        chain(0, middle, NLAT // 8, pair, state)
+        chain(1, lax.div(NLAT - HALF - place * HALF, 8), NLAT // 8, NLAT - 1 - pair)
+
+        right = lax.broadcasted_iota(jnp.int32, (16, 128), 1) < 64
+        blank = jnp.zeros((TROWS - ROWS // 2, 640), bf16)
+        for p in range(HALF):
+            for q in range(2):
+
+                def convert(t, carry):
+                    out = pl.ds(pl.multiple_of(t * 16, 16), 16)
+                    for tile in range(3):
+                        values = rows[tile, pl.ds(q * SIDE + t * 16 * PITCH + p, 16, stride=PITCH), :]
+                        high = values.astype(bf16)
+                        low = values - high.astype(f32)
+                        if tile < 2:
+                            at = tile * 128
+                            table_ref[p * 2 + q, out, at : at + 128] = high
+                            table_ref[p * 2 + q, out, at + 256 : at + 384] = low.astype(bf16)
+                        else:
+                            table_ref[p * 2 + q, out, 512:640] = jnp.where(right, values, low).astype(bf16)
+                    return carry
+
+                lax.fori_loop(0, ROWS // 32, convert, 0, unroll=3)
+                table_ref[p * 2 + q, ROWS // 2 : TROWS, :] = blank
+
+    return start, finish
 
 
 def spectral_kernel(
     prior_ref,
     post_ref,
-    lats_ref,
+    natural_ref,
     relax_ref,
     lead_hbm,
     high_hbm,
@@ -178,6 +190,7 @@
     trig_low,
     left,
     split,
+    lats_ref,
     out_a,
     out_b,
     in_a,
@@ -192,8 +205,7 @@
     summed,
     own,
     at_m,
-    at_y,
-    at_z,
+    at_g,
     ratio,
     merged,
     ret_a,
@@ -209,8 +221,6 @@
     r_p1,
     s_p2,
     r_p2,
-    s_p3,
-    r_p3,
     s_p4,
     r_p4,
     s_re,
@@ -259,6 +269,94 @@
             for h in range(2):
                 sums[ens * 20 + j * 2 + h] = ref[j, h, 0] + ref[j, h, 1]
     left[...] = jnp.zeros_like(left)
+
+    def fill(make):
+        for ens in range(2):
+            for j in range(HALF):
+                north, south = make(ens, j)
+                for q, part in ((0, north + south), (1, north - south)):
+                    for v in range(LEV):
+                        row = (ens * 4 + v * 2 + q) * 16 + j
+                        left[row : row + 1, :] = part[v : v + 1, :]
+        high, low = split_rows(left[...])
+        split[0:128, :] = high
+        split[128:256, :] = low
+
+    def fourier(half):
+        columns = pl.ds(pl.multiple_of(half * 640, 128), 640)
+        both = jnp.dot(split[...], trig_high[:, columns], preferred_element_type=f32)
+        return (
+            both[0:128]
+            + both[128:256]
+            + jnp.dot(split[0:128, :], trig_low[:, columns], preferred_element_type=f32)
+        )
+
+    def pieces(result, o):
+        return [result[x * 16 : x * 16 + 16, o * 40 : o * 40 + 40] for x in range(8)]
+
+    own_half = lax.div(y, 2)
+    targets = []
+    for step in range(2):
+        half = own_half if step == 0 else 1 - own_half
+        for j in range(2):
+            if step == 0:
+                far_y = y if j == 0 else y + 1 - 2 * lax.rem(y, 2)
+            else:
+                far_y = 2 * half + lax.rem(y + j, 2)
+            for dz in (4, 3, 5, 2, 6, 1, 7, 0):
+                if step == 0 and j == 0 and dz == 0:
+                    continue
+                targets.append((step, (step * 2 + j) * 8 + dz, far_y * NZ + lax.rem(z + dz, NZ)))
+
+    def give(part, k, peer, columns):
+        return [
+            send(
+                out_a.at[eight(peer), columns],
+                in_a.at[eight(me), columns],
+                s_ex.at[part, k],
+                r_ex.at[part, k],
+                {"grid": peer},
+            ),
+            send(
+                out_b.at[peer, :, columns],
+                in_b.at[me, :, columns],
+                s_ex.at[part + 1, k],
+                r_ex.at[part + 1, k],
+                {"grid": peer},
+            ),
+        ]
+
+    def difference(ens, j):
+        ref = (prior_ref, post_ref)[ens]
+        return tuple((ref[j, h, 0] - ref[j, h, 1]) * 0.5 for h in range(2))
+
+    fill(difference)
+    for copy in loads:
+        copy.wait()
+    for half in range(2):
+        result = fourier(half)
+        for o in range(16):
+            block = jnp.concatenate(pieces(result, o), axis=1)
+            place = half * 16 + o
+            out_a[place * 8 : place * 8 + 8, 0:320] = block[0:8]
+            out_b[place, :, 0:320] = block[8:10]
+
+    source = lax.broadcasted_iota(jnp.int32, (TROWS, TROWS), 0)
+    target = lax.broadcasted_iota(jnp.int32, (TROWS, TROWS), 1)
+    small = (target - 256) & 63
+    wanted = jnp.where(
+        target < 256,
+        (target >> 3) * HALF + (target & 7),
+        (small >> 1) * HALF + 8 + (small & 1),
+    )
+    lats_ref[...] = jnp.dot(
+        natural_ref[...],
+        jnp.where(source == wanted, 1.0, 0.0).astype(f32),
+        precision=lax.Precision.HIGHEST,
+        preferred_element_type=f32,
+    )
+    legendre_start, legendre_finish = legendre_parts(me, lead, lats_ref, table, rows, EARLY)
+
     pl.semaphore_wait(barrier, NM + NG - 2)
     pending = []
     now = []
@@ -273,6 +371,9 @@
                 mem_peer(k),
             )
         )
+    exchanged = []
+    for _, k, peer in targets:
+        exchanged += give(0, k, peer, pl.ds(0, 256))
     value = sums[pl.ds(mem * 5, 5)]
     for k, copy in enumerate(now):
         copy.wait_recv()
@@ -284,67 +385,34 @@
         send(piece, mean_ref.at[pl.ds(mem * 5, 5)], s_ag.at[k - 1], r_ag.at[k - 1], mem_peer(k))
         for k in range(1, NM)
     ]
+    legendre_state = legendre_start()
     for copy in now:
         copy.wait_recv()
     pending += now
 
-    for ens, ref in ((0, prior_ref), (1, post_ref)):
-        for j in range(HALF):
-            north_mean = mean_ref[ens * 20 + j * 2]
-            south_mean = mean_ref[ens * 20 + j * 2 + 1]
-            for b in range(2):
-                north = ref[j, 0, b] - north_mean
-                south = ref[j, 1, b] - south_mean
-                for q, part in ((0, north + south), (1, north - south)):
-                    for v in range(LEV):
-                        row = (q * 8 + ens * 4 + b * 2 + v) * 16 + j
-                        left[row : row + 1, :] = part[v : v + 1, :]
-    high, low = split_rows(left[...])
-    split[0:256, :] = high
-    split[256:512, :] = low
-    for copy in loads:
-        copy.wait()
-    own_half = lax.div(y, 2)
-    exchanged = []
+    def centred(ens, j):
+        return tuple(
+            sums[ens * 20 + j * 2 + h] * 0.5 - mean_ref[ens * 20 + j * 2 + h] for h in range(2)
+        )
+
+    fill(centred)
     for step in range(2):
         half = own_half if step == 0 else 1 - own_half
-        columns = pl.ds(pl.multiple_of(half * 640, 128), 640)
-        both = jnp.dot(split[...], trig_high[:, columns], preferred_element_type=f32)
-        result = both[0:256] + both[256:512]
-        result = result + jnp.dot(
-            split[0:256, :], trig_low[:, columns], preferred_element_type=f32
-        )
+        result = fourier(half)
         for o in range(16):
-            block = jnp.concatenate(
-                [result[x * 16 : x * 16 + 16, o * 40 : o * 40 + 40] for x in range(16)], axis=1
-            )
             place = half * 16 + o
-            out_a[eight(place), :] = block[0:8]
-            out_b[place] = block[8:10]
-        for j in range(2):
-            if step == 0:
-                far_y = y if j == 0 else y + 1 - 2 * lax.rem(y, 2)
-            else:
-                far_y = 2 * half + lax.rem(y + j, 2)
-            for dz in (4, 3, 5, 2, 6, 1, 7, 0):
-                if step == 0 and j == 0 and dz == 0:
-                    continue
-                peer = far_y * NZ + lax.rem(z + dz, NZ)
-                k = (step * 2 + j) * 8 + dz
-                exchanged.append(
-                    send(
-                        out_a.at[eight(peer), :],
-                        in_a.at[eight(me), :],
-                        s_ex.at[0, k],
-                        r_ex.at[0, k],
-                        {"grid": peer},
-                    )
-                )
-                exchanged.append(
-                    send(out_b.at[peer], in_b.at[me], s_ex.at[1, k], r_ex.at[1, k], {"grid": peer})
-                )
-
-    build_legendre(me, lead, lats_ref, table, rows)
+            parts = pieces(result, o)
+            out_a[eight(place), 256:640] = jnp.concatenate(
+                [out_a[eight(place), 256:320]] + [part[0:8] for part in parts], axis=1
+            )
+            out_b[place, :, 256:640] = jnp.concatenate(
+                [out_b[place, :, 256:320]] + [part[8:10] for part in parts], axis=1
+            )
+        for at, k, peer in targets:
+            if at == step:
+                exchanged += give(2, k, peer, pl.ds(256, 384))
+
+    legendre_finish(legendre_state)
 
     in_a[eight(me), :] = out_a[eight(me), :]
     in_b[me] = out_b[me]
@@ -364,16 +432,16 @@
 
     def analyse_pair(p, odd):
         pair = me * HALF + p
-        first_weight = jnp.where(pair == 0, 1.0, 2.0).astype(f32)
+        first_weight = jnp.where(pair == 0, 2.0, 4.0).astype(f32)
         for q in range(2):
             groups = []
             for e in range(2):
                 parity = (q + odd + 1 - e) % 2
                 for part in range(2):
-                    start = parity * 320 + p * 4 + e * 2 + part
+                    start = parity * 40 + p * 4 + e * 2 + part
                     groups.append(
                         jnp.concatenate(
-                            [turned[t, pl.ds(start, 8, stride=40), :] for t in range(3)], axis=1
+                            [turned[t, pl.ds(start, 8, stride=80), :] for t in range(3)], axis=1
                         )
                     )
             high, low = split_rows(jnp.concatenate(groups, axis=0))
@@ -397,7 +465,7 @@
             squares = chosen * chosen
             where = slice(q * TROWS, (q + 1) * TROWS)
             total[0, :, where] += jnp.where(in_first, squares, 0.0) * first_weight
-            total[1, :, where] += jnp.where(in_first, 0.0, squares) * 2.0
+            total[1, :, where] += jnp.where(in_first, 0.0, squares) * 4.0
 
     def analyse_two(i, carry):
         analyse_pair(2 * i, 0)
@@ -407,9 +475,7 @@
     lax.fori_loop(0, HALF // 2, analyse_two, 0)
     for s in range(2):
         both = total[s, 0:8, :] + total[s, 8:16, :]
-        for ens in range(2):
-            row = s * 4 + ens * 2
-            power[row : row + 2, 0:768] = both[ens * 4 : ens * 4 + 2] + both[ens * 4 + 2 : ens * 4 + 4]
+        power[s * 4 : s * 4 + 4, 0:768] = both[0:4] + both[4:8]
     power[:, 768:1024] = jnp.zeros((8, 256), f32)
 
     def lanes(index):
@@ -431,24 +497,15 @@
         value = value + at_m[k]
     pending += now
 
-    def y_peer(k):
-        return {"grid": lax.rem(y + k, NY) * NZ + z}
-
-    def z_peer(k):
-        return {"grid": y * NZ + lax.rem(z + k, NZ)}
-
-    for stage, (peer, count, sends, receives, slots) in enumerate(
-        ((y_peer, NY, s_p2, r_p2, at_y), (z_peer, NZ, s_p3, r_p3, at_z))
-    ):
-        own[stage] = value
-        now = [
-            send(own.at[stage], slots.at[k - 1], sends.at[k - 1], receives.at[k - 1], peer(k))
-            for k in range(1, count)
-        ]
-        for k, copy in enumerate(now):
-            copy.wait_recv()
-            value = value + slots[k]
-        pending += now
+    own[0] = value
+    now = [
+        send(own.at[0], at_g.at[k - 1], s_p2.at[k - 1], r_p2.at[k - 1], {"grid": peer_of(k)})
+        for k in sorted(range(1, NG), key=lambda k: -min(k % NZ, NZ - k % NZ))
+    ]
+    for copy in now:
+        copy.wait_recv()
+    value = value + jnp.sum(at_g[...], axis=0)
+    pending += now
     own[2] = value
     summed[:, lanes(mem)] = value
     now = [
@@ -514,12 +571,13 @@
             for e in range(2):
                 parity = (q + odd + 1 - e) % 2
                 for part in range(2):
-                    at = e * 16 + part * 8 + 4
-                    start = parity * 160 + p * 4 + e * 2 + part
-                    where = pl.ds(start, 4, stride=40)
-                    merged[0, where, :] = a_part[at : at + 4, 0:128]
-                    merged[1, where, :] = a_part[at : at + 4, 128:256]
-                    merged[2, where, :] = b_part[at : at + 4]
+                    for b in range(2):
+                        at = e * 16 + part * 8 + b * 4 + 2
+                        start = (parity * 4 + b * 2) * 40 + p * 4 + e * 2 + part
+                        where = pl.ds(start, 2, stride=40)
+                        merged[0, where, :] = a_part[at : at + 2, 0:128]
+                        merged[1, where, :] = a_part[at : at + 2, 128:256]
+                        merged[2, where, :] = b_part[at : at + 2]
 
     def synth_two(i, carry):
         synth_pair(2 * i, 0)
@@ -557,7 +615,7 @@
         copy.wait_send()
 
 
-def spectral(prior, posterior, lats, relaxation, lead, high, low):
+def spectral(prior, posterior, natural, relaxation, lead, high, low):
     vmem = pl.BlockSpec(memory_space=pltpu.VMEM)
     hbm = pl.BlockSpec(memory_space=pl.ANY)
     return pl.pallas_call(
@@ -576,8 +634,9 @@
             pltpu.VMEM((2, 16, 128), f32),
             pltpu.VMEM((NLON, NLON), bf16),
             pltpu.VMEM((NLON, NLON), bf16),
-            pltpu.VMEM((256, NLON), f32),
-            pltpu.VMEM((512, NLON), bf16),
+            pltpu.VMEM((128, NLON), f32),
+            pltpu.VMEM((256, NLON), bf16),
+            pltpu.VMEM((8, TROWS), f32),
             pltpu.VMEM((NG * 8, 640), f32),
             pltpu.VMEM((NG, 2, 640), f32),
             pltpu.VMEM((NG * 8, 640), f32),
@@ -592,8 +651,7 @@
             pltpu.VMEM((8, 1024), f32),
             pltpu.VMEM((3, 8, 128), f32),
             pltpu.VMEM((NM - 1, 8, 128), f32),
-            pltpu.VMEM((NY - 1, 8, 128), f32),
-            pltpu.VMEM((NZ - 1, 8, 128), f32),
+            pltpu.VMEM((NG - 1, 8, 128), f32),
             pltpu.VMEM((2, 2, 16, TROWS), f32),
             pltpu.VMEM((3, TROWS, 128), f32),
             pltpu.VMEM((NG * 8, TROWS), f32),
@@ -601,14 +659,14 @@
             pltpu.SemaphoreType.DMA((3,)),
         ]
         + [pltpu.SemaphoreType.DMA((NM - 1,)) for _ in range(4)]
-        + [pltpu.SemaphoreType.DMA((2, NG)) for _ in range(2)]
-        + [pltpu.SemaphoreType.DMA((n - 1,)) for n in (NM, NM, NY, NY, NZ, NZ, NM, NM)]
+        + [pltpu.SemaphoreType.DMA((4, NG)) for _ in range(2)]
+        + [pltpu.SemaphoreType.DMA((n - 1,)) for n in (NM, NM, NG, NG, NM, NM)]
         + [pltpu.SemaphoreType.DMA((2, NG)) for _ in range(2)],
         compiler_params=pltpu.CompilerParams(
             collective_id=0, has_side_effects=True, vmem_limit_bytes=BIG
         ),
         name="spectral",
-    )(prior, posterior, lats, relaxation, lead, high, low)
+    )(prior, posterior, natural, relaxation, lead, high, low)
 
 
 def inverse_kernel(src_a, src_b, mean_ref, high_ref, low_ref, out_ref, split, joined):
@@ -636,12 +694,15 @@
     north = result[0:64] + result[64:128]
     south = result[0:64] - result[64:128]
     for h, part in ((0, north), (1, south)):
+        members = (part[32:64] + part[0:32], part[32:64] - part[0:32])
         for j in range(HALF):
             mean = mean_ref[20 + j * 2 + h]
             for b in range(2):
                 for v in range(LEV):
-                    row = (b * 2 + v) * 16 + j
-                    out_ref[j, h, b, v : v + 1, :] = part[row : row + 1, :] + mean[v : v + 1, :]
+                    row = v * 16 + j
+                    out_ref[j, h, b, v : v + 1, :] = (
+                        members[b][row : row + 1, :] + mean[v : v + 1, :]
+                    )
 
 
 def inverse_fourier(returned, mean, high, low):
@@ -664,18 +725,12 @@
     )(*returned, mean, high, low)
 
 
-def lane_order():
-    grouped = np.arange(NPAIR).reshape(NG, HALF)
-    two = grouped[:, 8:10].reshape(-1)
-    return np.concatenate([grouped[:, 0:8].reshape(-1), two, two]).astype(np.int32)
-
-
 def per_device(prior, posterior, cycle_rows, relaxation):
     forward_high, forward_low, inverse_high, inverse_low = (jnp.asarray(t) for t in trig_tables())
-    rows = jnp.take(cycle_rows, jnp.asarray(lane_order()))
-    colatitude = math.pi * (rows.astype(f32) + 0.5) / NLAT
+    colatitude = math.pi * (cycle_rows.reshape(1, NPAIR).astype(f32) + 0.5) / NLAT
     sines = jnp.sin(colatitude)
-    lats = jnp.stack([jnp.cos(colatitude), math.pi / NLAT * sines, jnp.log(sines)])
+    lats = jnp.concatenate([jnp.cos(colatitude), math.pi / NLAT * sines, jnp.log(sines)], axis=0)
+    lats = jnp.pad(lats, ((0, 5), (0, TROWS - NPAIR)))
     mean, back_a, back_b = spectral(
         prior, posterior, lats, relaxation, jnp.asarray(leading_logs()), forward_high, forward_low
     )

time: 101 us -> 90.8 us (0.90)
  Pallas kernels: 96.2 us -> 89.3 us
  local copies, waits for them, and re-layouts: 2.8 us -> 0.01 us
    pallas_call x1, Pallas kernels: 90.1 us -> 83.2 us  [spectral(): pl.pallas_call(spectral_kernel, out_shape=(jax.ShapeDtypeStruct((40, LEV,...]
    gather x1 -> x0, local copies, waits for them, and re-layouts: 2.79 us -> none  [per_device(): rows = jnp.take(cycle_rows, jnp.asarray(lane_order()))]
where the time goes in v3:
time: 90.8 us; the launch traced here: 90.7 us
  Pallas kernels  89.3 us (98%)
  other arithmetic  1.34 us (1%)
    pallas_call x1, Pallas kernels, spectral(): pl.pallas_call(spectral_kernel, out_shape=(jax.ShapeDtypeStruct((40, LEV,...  83.2 us
    pallas_call x1, Pallas kernels, inverse_fourier(): pl.pallas_call(inverse_kernel, grid=(NLON // width,), out_shape=jax.Shape...  6.14 us

profile of v3, /device:TPU:1, one launch (start us, length us, event | category | flops | bytes accessed | tf_op | source)
XLA Modules:
  0.0 90.7 jit_solution(1464300021907102701)
XLA Ops:
  0.0 0.7 fusion.1
  0.8 0.6 select_maximum_fusion.natural_ref
  1.4 83.2 %spectral.1 = (f32[40,2,1280]{2,1,0:T(2,128)}, f32[256,384]{1,0:T(8,128)}, f32[32,2,384]{2,1,0:T(2,128)}) custom-call(f32[10,2,2,2,1280]{4,3,2,1,0:T(2,128)} %prior_ref.1, f32[10,2,2,2,1280]{4,3,2,1,0:T(2,128)} %post_ref.1, f32[8,384]{1,0:T(8,128)} %select_maximum_fusion.natural_ref, f32[2]{0:T(128)} %relax_ref.1, ...), custom_call_target="tpu_custom_call" | custom-call | tf_op jit(solution)/shard_map/spectral/pallas_call | solution.py:621
  84.6 6.1 %inverse_fourier.1 = f32[10,2,2,2,1280]{4,3,2,1,0:T(2,128)} custom-call(f32[256,384]{1,0:T(8,128)} %get-tuple-element.8.src_a, f32[32,2,384]{2,1,0:T(2,128)} %get-tuple-element.9.src_b, f32[40,2,1280]{2,1,0:T(2,128)} %get-tuple-element.10.mean_ref, bf16[1280,1280]{1,0:T(8,128)(2,1)} %constant.23.clone.high_ref, bf16[1280,1280]{1,0:T(8,128)(2,1)} %constant.24.clone.low_ref), custom_call_target="tpu_custom_call" | custom-call | tf_op jit(solution)/shard_map/inverse_fourier/pallas_call | solution.py:710
  (3 shorter events, 0.0 us)

commit v4 on v3

--- a/solution.py
+++ b/solution.py
@@ -210,6 +210,8 @@
     merged,
     ret_a,
     ret_b,
+    packed,
+    last,
     local_sem,
     s_rs,
     r_rs,
@@ -586,11 +588,26 @@
 
     merged[:, 320:384, :] = jnp.zeros((3, 64, 128), f32)
     lax.fori_loop(0, HALF // 2, synth_two, 0)
+    b_rows = merged[2].T[0:64]
+    for c in range(4):
+        tile = b_rows[:, (c // 2) * 128 : (c // 2) * 128 + 128]
+        packed[pl.ds(c, 64, stride=4), :] = tile if c % 2 else pltpu.roll(tile, 64, 1)
+    last[...] = b_rows[:, 256:384]
+    left_half = lax.broadcasted_iota(jnp.int32, (128, 128), 1) < 64
+    ends = jnp.where(
+        left_half[0:NG],
+        last[pl.ds(0, NG, stride=2), :],
+        pltpu.roll(last[pl.ds(1, NG, stride=2), :], 64, 1),
+    )
+    for g in range(NG):
+        ret_b[g] = ends[g : g + 1, :]
     for t in range(2):
-        ret_a[t * 128 : t * 128 + 128, :] = merged[t].T
-    b_rows = merged[2].T
-    for g in range(NG):
-        ret_b[g] = b_rows[g * 2 : g * 2 + 2, :]
+        at = t * 128
+        a_rows = merged[t].T
+        ret_a[at : at + 128, 0:256] = a_rows[:, 0:256]
+        ret_a[at : at + 128, 256:384] = jnp.where(
+            left_half, a_rows[:, 256:384], packed[at : at + 128, :]
+        )
 
     now = []
     for k in sorted(range(1, NG), key=lambda k: -min(k % NZ, NZ - k % NZ)):
@@ -623,7 +640,7 @@
         out_shape=(
             jax.ShapeDtypeStruct((40, LEV, NLON), f32),
             jax.ShapeDtypeStruct((NG * 8, TROWS), f32),
-            jax.ShapeDtypeStruct((NG, 2, TROWS), f32),
+            jax.ShapeDtypeStruct((NG, 1, 128), f32),
         ),
         in_specs=[vmem, vmem, vmem, pl.BlockSpec(memory_space=pltpu.SMEM), hbm, hbm, hbm],
         out_specs=(vmem, vmem, vmem),
@@ -655,7 +672,9 @@
             pltpu.VMEM((2, 2, 16, TROWS), f32),
             pltpu.VMEM((3, TROWS, 128), f32),
             pltpu.VMEM((NG * 8, TROWS), f32),
-            pltpu.VMEM((NG, 2, TROWS), f32),
+            pltpu.VMEM((NG, 1, 128), f32),
+            pltpu.VMEM((256, 128), f32),
+            pltpu.VMEM((64, 128), f32),
             pltpu.SemaphoreType.DMA((3,)),
         ]
         + [pltpu.SemaphoreType.DMA((NM - 1,)) for _ in range(4)]
@@ -669,12 +688,29 @@
     )(prior, posterior, natural, relaxation, lead, high, low)
 
 
-def inverse_kernel(src_a, src_b, mean_ref, high_ref, low_ref, out_ref, split, joined):
+def inverse_kernel(
+    src_a, src_b, mean_ref, high_ref, low_ref, out_ref, split, joined, spread, both_rows
+):
     @pl.when(pl.program_id(0) == 0)
     def _():
+        spread[...] = src_a[:, 256:384]
+        left_half = lax.broadcasted_iota(jnp.int32, (64, 128), 1) < 64
+        found = [spread[pl.ds(c, 64, stride=4), :] for c in range(4)]
+        for o in range(NG):
+            end = src_b[o]
+            both_rows[o * 2 : o * 2 + 1, :] = end
+            both_rows[o * 2 + 1 : o * 2 + 2, :] = pltpu.roll(end, 64, 1)
+        b_rows = jnp.concatenate(
+            [
+                jnp.where(left_half, pltpu.roll(found[0], 64, 1), found[1]),
+                jnp.where(left_half, pltpu.roll(found[2], 64, 1), found[3]),
+                both_rows[...],
+            ],
+            axis=1,
+        )
         for o in range(NG):
             joined[o * 16 : o * 16 + 8, :] = src_a[o * 8 : o * 8 + 8, :]
-            joined[o * 16 + 8 : o * 16 + 10, :] = src_b[o]
+            joined[o * 16 + 8 : o * 16 + 10, :] = b_rows[o * 2 : o * 2 + 2, :]
             joined[o * 16 + 10 : o * 16 + 16, :] = jnp.zeros((6, TROWS), f32)
         for x in range(8):
             row = jnp.concatenate(
@@ -713,13 +749,18 @@
         out_shape=jax.ShapeDtypeStruct((HALF, 2, 2, LEV, NLON), f32),
         in_specs=[
             pl.BlockSpec((NG * 8, TROWS), lambda i: (0, 0)),
-            pl.BlockSpec((NG, 2, TROWS), lambda i: (0, 0, 0)),
+            pl.BlockSpec((NG, 1, 128), lambda i: (0, 0, 0)),
             pl.BlockSpec((40, LEV, width), lambda i: (0, 0, i)),
             pl.BlockSpec((NLON, width), lambda i: (0, i)),
             pl.BlockSpec((NLON, width), lambda i: (0, i)),
         ],
         out_specs=pl.BlockSpec((HALF, 2, 2, LEV, width), lambda i: (0, 0, 0, 0, i)),
-        scratch_shapes=[pltpu.VMEM((256, NLON), bf16), pltpu.VMEM((NG * 16, TROWS), f32)],
+        scratch_shapes=[
+            pltpu.VMEM((256, NLON), bf16),
+            pltpu.VMEM((NG * 16, TROWS), f32),
+            pltpu.VMEM((256, 128), f32),
+            pltpu.VMEM((64, 128), f32),
+        ],
         compiler_params=pltpu.CompilerParams(vmem_limit_bytes=BIG),
         name="inverse_fourier",
     )(*returned, mean, high, low)

time: 90.8 us -> 89.2 us (0.982)
  Pallas kernels: 89.3 us -> 87.7 us
    pallas_call x1, Pallas kernels: 83.2 us -> 81.5 us  [spectral(): pl.pallas_call(spectral_kernel, out_shape=(jax.ShapeDtypeStruct((40, LEV,...]
where the time goes in v4:
time: 89.2 us; the launch traced here: 89.1 us
  Pallas kernels  87.7 us (98%)
  other arithmetic  1.34 us (2%)
    pallas_call x1, Pallas kernels, spectral(): pl.pallas_call(spectral_kernel, out_shape=(jax.ShapeDtypeStruct((40, LEV,...  81.5 us
    pallas_call x1, Pallas kernels, inverse_fourier(): pl.pallas_call(inverse_kernel, grid=(NLON // width,), out_shape=jax.Shape...  6.23 us

profile of v4, /device:TPU:1, one launch (start us, length us, event | category | flops | bytes accessed | tf_op | source)
XLA Modules:
  0.0 89.1 jit_solution(16970917910925398113)
XLA Ops:
  0.0 0.7 fusion.1
  0.8 0.6 select_maximum_fusion.natural_ref
  1.4 81.5 %spectral.1 = (f32[40,2,1280]{2,1,0:T(2,128)}, f32[256,384]{1,0:T(8,128)}, f32[32,1,128]{2,1,0:T(1,128)}) custom-call(f32[10,2,2,2,1280]{4,3,2,1,0:T(2,128)} %prior_ref.1, f32[10,2,2,2,1280]{4,3,2,1,0:T(2,128)} %post_ref.1, f32[8,384]{1,0:T(8,128)} %select_maximum_fusion.natural_ref, f32[2]{0:T(128)} %relax_ref.1, ...), custom_call_target="tpu_custom_call" | custom-call | tf_op jit(solution)/shard_map/spectral/pallas_call | solution.py:638
  82.9 6.2 %inverse_fourier.1 = f32[10,2,2,2,1280]{4,3,2,1,0:T(2,128)} custom-call(f32[256,384]{1,0:T(8,128)} %get-tuple-element.8.src_a, f32[32,1,128]{2,1,0:T(1,128)} %get-tuple-element.9.src_b, f32[40,2,1280]{2,1,0:T(2,128)} %get-tuple-element.10.mean_ref, bf16[1280,1280]{1,0:T(8,128)(2,1)} %constant.23.clone.high_ref, bf16[1280,1280]{1,0:T(8,128)(2,1)} %constant.24.clone.low_ref), custom_call_target="tpu_custom_call" | custom-call | tf_op jit(solution)/shard_map/inverse_fourier/pallas_call | solution.py:746
  (3 shorter events, 0.0 us)
